TPU v7x, 128 devices: a whole 4x4x4 slice. The times are simulated.
128 devices in a mesh: rows: 16 (over x, y_hi, core), frames: 8 (over y_lo, z).
Axes of the slice: x: 4, y: 4 (y_hi: 2, y_lo: 2; y = y_hi * 2 + y_lo), z: 4, core: 2. Of those that a mesh axis runs over, the one named last changes fastest.
Arguments:
- latent: bfloat16 [128, 1664, 256], P('frames', 'rows'), may hold values from -25 to 25
- conv_weight: bfloat16 [4, 256, 256], replicated, may hold values from -0.25 to 0.25
- norm_gain: bfloat16 [256], replicated, may hold values from 0.099609375 to 1.8984375
- frame_embed: bfloat16 [256, 256], P('frames'), may hold values from -3 to 3
- qkv_weight: bfloat16 [256, 768], replicated, may hold values from -3 to 3
- out_weight: bfloat16 [256, 256], replicated, may hold values from -0.375 to 0.375
Outputs:
- blended: bfloat16 [256, 1664, 256], P('frames', 'rows')
All inputs are finite; a program needn't handle non-finite values.
Results may differ from a plain program's by a relative error of at most 0.0095.
The roundings to bfloat16 on the way count: a program that leaves them out, or rounds other values in their place, can miss the bound.
Values may be sent and summed in bfloat16 or wider, within the bound.
No kernel may reach another device: no remote copies, remote signals or barrier semaphores. Data moves between devices by JAX's collectives and lax.ppermute only.
A program may use at most 64 MiB of HBM per device.

v0:
```python
import jax
import jax.numpy as jnp
from jax import lax
from jax.sharding import PartitionSpec as P

HEAD_DIM = 64
GROUPS = 32


epsilon = 1e-06


def extended(cells, sides, width):
    for axis, dim in sides:
        count = lax.axis_size(axis)
        ends = count - 1
        head = lax.slice_in_dim(cells, 0, width, axis=dim)
        tail = lax.slice_in_dim(cells, cells.shape[dim] - width, cells.shape[dim], axis=dim)
        cells = jnp.concatenate(
            [
                lax.ppermute(tail, axis, [(i, (i + 1) % count) for i in range(ends)]),
                cells,
                lax.ppermute(head, axis, [((i + 1) % count, i) for i in range(ends)]),
            ],
            axis=dim,
        )
    return cells


def shortened(array):

    def short(part):
        return part.astype(jnp.bfloat16) if part.dtype == jnp.float32 else part

    return jax.tree.map(short, array)


def attend_pixel(projected):
    channels = projected.shape[-1] // 3
    length = projected.shape[0]
    queries = projected[:, :channels].reshape(length, channels // HEAD_DIM, HEAD_DIM)
    keys = projected[:, channels : 2 * channels].reshape(length, channels // HEAD_DIM, HEAD_DIM)
    values = projected[:, 2 * channels :].reshape(length, channels // HEAD_DIM, HEAD_DIM)
    scores = jnp.einsum(
        "qhd,khd->hqk", queries, keys, preferred_element_type=jnp.float32
    ) * HEAD_DIM ** (-0.5)
    scores = scores - jnp.max(scores, axis=-1, keepdims=True)
    weights = jnp.exp(scores)
    probabilities = (weights / jnp.sum(weights, axis=-1, keepdims=True)).astype(jnp.bfloat16)
    context = jnp.einsum("hqk,khd->qhd", probabilities, values, preferred_element_type=jnp.float32)
    return context.reshape(length, channels).astype(jnp.bfloat16)


def normalize(upsampled_float, norm_gain, embed_rows):
    channels = upsampled_float.shape[-1]
    group_size = channels // GROUPS
    counted = (
        upsampled_float.shape[0]
        * upsampled_float.shape[1]
        * group_size
        * lax.axis_size("rows")
        * lax.axis_size("frames")
    )

    def by_group(column_sums):
        return column_sums.reshape(GROUPS, group_size).sum(axis=1)

    group_total = lax.psum(by_group(jnp.sum(upsampled_float, axis=(0, 1))), ("rows", "frames"))
    center = group_total / counted
    channel_center = jnp.repeat(center, group_size)
    centered = upsampled_float - channel_center
    deviation = lax.psum(by_group(jnp.sum(centered * centered, axis=(0, 1))), ("rows", "frames"))
    variance = deviation / counted
    channel_scale = jnp.repeat(lax.rsqrt(variance + epsilon), group_size) * norm_gain.astype(
        jnp.float32
    )
    return (centered * channel_scale + embed_rows.astype(jnp.float32)[:, None, :]).astype(
        jnp.bfloat16
    )


def per_device(latent, conv_weight, norm_gain, frame_embed, qkv_weight, out_weight):
    frames_local = latent.shape[0]
    pixels_local = latent.shape[1]
    channels = latent.shape[2]
    out_local = 2 * frames_local
    frame_devices = lax.axis_size("frames")
    pixel_share = pixels_local // frame_devices

    def apply_tap(piece, index):
        return jnp.einsum(
            "fpc,cd->fpd", piece, conv_weight[index], preferred_element_type=jnp.float32
        )

    padded = extended(latent, (("frames", 0),), 1)
    even_frames = apply_tap(padded[1:-1], 1) + apply_tap(padded[:-2], 3)
    odd_frames = apply_tap(padded[2:], 0) + apply_tap(padded[1:-1], 2)
    upsampled = (
        jnp.stack([even_frames, odd_frames], axis=1)
        .reshape(out_local, pixels_local, channels)
        .astype(jnp.bfloat16)
    )
    upsampled_float = upsampled.astype(jnp.float32)
    normed = normalize(upsampled_float, norm_gain, frame_embed)
    projected = jnp.einsum(
        "fpc,cd->fpd", normed, qkv_weight, preferred_element_type=jnp.float32
    ).astype(jnp.bfloat16)
    per_pixel = jnp.moveaxis(
        lax.all_to_all(
            projected.reshape(out_local, frame_devices, pixel_share, 3 * channels),
            "frames",
            split_axis=1,
            concat_axis=0,
            tiled=True,
        )[:, 0],
        1,
        0,
    )
    context = lax.map(attend_pixel, per_pixel, batch_size=4)
    context = jnp.moveaxis(context, 0, 1)[:, None]
    returned = (
        lax.all_to_all(shortened(context), "frames", split_axis=0, concat_axis=1, tiled=True)
        .astype(context.dtype)
        .reshape(out_local, pixels_local, channels)
    )
    blended = upsampled_float + jnp.einsum(
        "fpc,cd->fpd", returned, out_weight, preferred_element_type=jnp.float32
    )
    return blended.astype(jnp.bfloat16)


def solution(mesh):
    return jax.shard_map(
        per_device,
        mesh=mesh,
        in_specs=(P("frames", "rows", None), P(), P(), P("frames", None), P(), P()),
        out_specs=P("frames", "rows", None),
        check_vma=False,
    )
```

profile of v0, /device:TPU:0, one launch (start us, length us, event | category | flops | bytes accessed | tf_op | source)
XLA Modules:
  0.0 300.0 jit_solution(5072795526163333083)
XLA Ops:
  2.3 4.5 %collective-permute-start = (bf16[1,104,256]{2,1,0:T(8,128)(2,1)S(1)}, bf16[1,104,256]{2,1,0:T(8,128)(2,1)S(1)}, u32[]{:S(2)}, u32[]{:S(2)}) collective-permute-start(bf16[1,104,256]{2,1,0:T(8,128)(2,1)S(1)} %get-tuple-element.46), channel_id=1, source_target_pairs={{0,1},{1,2},{2,3},{3,4},{4,5},{5,6},{6,7},{8,9},{9,10},{10,11},{11... | collective-permute-start | bytes 159752 | tf_op jit(solution)/shard_map/ppermute | solution.py:21
  6.8 1.5 fusion.27
  10.3 71.1 %psum.14 = f32[32]{0:T(128)S(1)} all-reduce(f32[32]{0:T(128)S(1)} %reduce_sum.55), channel_id=1, replica_groups=mesh['rows'=16,'frames'=8] {'rows','frames'}, use_global_device_ids=true, to_apply=%region_2.0 | all-reduce | flops 32 | bytes 256 | tf_op jit(solution)/shard_map/psum | solution.py:68
  82.3 2.0 fusion.15
  84.2 62.3 %psum.15 = f32[32]{0:T(128)S(1)} all-reduce(f32[32]{0:T(128)S(1)} %reduce_sum.57), channel_id=1, replica_groups=mesh['rows'=16,'frames'=8] {'rows','frames'}, use_global_device_ids=true, to_apply=%region_5.0 | all-reduce | flops 32 | bytes 256 | tf_op jit(solution)/shard_map/psum | solution.py:72
  146.8 2.3 copy.37
  149.2 1.8 copy-done.1
  153.0 3.5 %copy.38 = bf16[32,104,768]{2,0,1:T(8,128)(2,1)} copy(bf16[32,104,768]{2,1,0:T(8,128)(2,1)S(1)} %convolution_convert_fusion) | data formatting | bytes 10223616 | tf_op jit(solution)/shard_map/convert_element_type | solution.py:107
  156.4 4.8 %all-to-all-start = ((bf16[32,8,13,768]{3,0,2,1:T(8,128)(2,1)}), bf16[32,8,13,768]{3,0,2,1:T(8,128)(2,1)}, u32[]{:S(2)}, u32[]{:S(2)}) async-start(bf16[32,8,13,768]{3,0,2,1:T(8,128)(2,1)} %bitcast.103), calls=%async_computation | async-start | bytes 10223616 | tf_op jit(solution)/shard_map/all_to_all | solution.py:109
  161.3 58.5 %all-to-all-done = bf16[32,8,13,768]{3,0,2,1:T(8,128)(2,1)} async-done(((bf16[32,8,13,768]{3,0,2,1:T(8,128)(2,1)}), bf16[32,8,13,768]{3,0,2,1:T(8,128)(2,1)}, u32[]{:S(2)}, u32[]{:S(2)}) %all-to-all-start) | async-done | bytes 5111840 | tf_op jit(solution)/shard_map/all_to_all | solution.py:109
  219.7 3.0 copy.39
  222.7 2.2 copy-done.3
  226.1 4.8 %slice.66 = bf16[12,256,768]{2,1,0:T(8,128)(2,1)} slice(bf16[13,256,768]{2,1,0:T(8,128)(2,1)} %bitcast.102), slice={[0:12], [0:256], [0:768]} | slice | bytes 9437184 | tf_op jit(solution)/shard_map/slice | solution.py:119
  232.2 28.5 %while.10 = (s32[]{:T(128)}, bf16[3,4,256,256]{3,2,1,0:T(8,128)(2,1)}, bf16[3,4,256,768]{3,2,1,0:T(8,128)(2,1)}, s32[]{:T(128)}) while((s32[]{:T(128)}, bf16[3,4,256,256]{3,2,1,0:T(8,128)(2,1)}, bf16[3,4,256,768]{3,2,1,0:T(8,128)(2,1)}, s32[]{:T(128)}) %tuple.34), condition=%wide.region_9.10_spmd, body=%wide.region_6.9_spmd.sunk | while | flops 273940736 | bytes 22053432 | solution.py:119
  234.5 3.4 %fusion.71 = (f32[4,4,256]{2,1,0:T(4,128)S(1)}, f32[4,4,256,256]{2,3,1,0:T(8,128)}) fusion(bf16[4,256,4,64]{1,3,2,0:T(8,128)(2,1)S(1)} %bitcast.107, bf16[4,256,4,64]{1,3,2,0:T(8,128)(2,1)S(1)} %bitcast.106), kind=kOutput, calls=%fused_computation.59.clone.1 | convolution fusion | flops 137363712 | bytes 5259264 | tf_op jit(solution)/shard_map/while/body/eval_jaxpr/vmap()/sub | solution.py:47
  238.0 2.7 fusion.72
  244.0 3.4 %fusion.71 = (f32[4,4,256]{2,1,0:T(4,128)S(1)}, f32[4,4,256,256]{2,3,1,0:T(8,128)}) fusion(bf16[4,256,4,64]{1,3,2,0:T(8,128)(2,1)S(1)} %bitcast.107, bf16[4,256,4,64]{1,3,2,0:T(8,128)(2,1)S(1)} %bitcast.106), kind=kOutput, calls=%fused_computation.59.clone.1 | convolution fusion | flops 137363712 | bytes 5259264 | tf_op jit(solution)/shard_map/while/body/eval_jaxpr/vmap()/sub | solution.py:47
  247.4 2.7 fusion.72
  253.5 3.4 %fusion.71 = (f32[4,4,256]{2,1,0:T(4,128)S(1)}, f32[4,4,256,256]{2,3,1,0:T(8,128)}) fusion(bf16[4,256,4,64]{1,3,2,0:T(8,128)(2,1)S(1)} %bitcast.107, bf16[4,256,4,64]{1,3,2,0:T(8,128)(2,1)S(1)} %bitcast.106), kind=kOutput, calls=%fused_computation.59.clone.1 | convolution fusion | flops 137363712 | bytes 5259264 | tf_op jit(solution)/shard_map/while/body/eval_jaxpr/vmap()/sub | solution.py:47
  256.9 2.7 fusion.72
  260.7 1.6 maximum_bitcast_fusion
  263.3 30.8 %all_to_all.30 = bf16[256,1,13,256]{3,2,1,0:T(8,128)(2,1)S(1)} all-to-all(bf16[256,1,13,256]{3,2,1,0:T(8,128)(2,1)S(1)} %copy.47), channel_id=1, replica_groups=mesh['rows'=16,'frames'=8] {'frames'}, dimensions={0} | all-to-all | bytes 3407872 | tf_op jit(solution)/shard_map/all_to_all | solution.py:122
  295.0 1.7 copy-done.2
  296.7 3.3 %fusion.14 = bf16[32,104,256]{2,1,0:T(8,128)(2,1)} fusion(f32[16,2,104,256]{3,2,1,0:T(8,128)S(1)} %copy-done.2, bf16[32,104,256]{2,0,1:T(8,128)(2,1)S(1)} %bitcast.109, bf16[256,256]{1,0:T(8,128)(2,1)S(1)} %copy-done.6), kind=kOutput, calls=%fused_computation.19 | convolution fusion | flops 437911552 | bytes 6946816 | tf_op jit(solution)/shard_map/fpc,cd->fpd/dot_general | solution.py:126
  (65 shorter events, 21.4 us)
Async XLA Ops:
  0.0 151.5 %copy-start = (bf16[256,768]{1,0:T(8,128)(2,1)S(1)}, bf16[256,768]{1,0:T(8,128)(2,1)}, u32[]{:S(2)}) copy-start(bf16[256,768]{1,0:T(8,128)(2,1)} %param.12) | copy-start | bytes 1179652
  0.0 8.4 %copy-start.4 = (bf16[16,104,256]{2,1,0:T(8,128)(2,1)S(1)}, bf16[16,104,256]{2,1,0:T(8,128)(2,1)}, u32[]{:S(2)}) copy-start(bf16[16,104,256]{2,1,0:T(8,128)(2,1)} %param.8) | copy-start | bytes 2555908
  0.0 8.4 %copy-start.5 = (bf16[4,256,256]{2,1,0:T(8,128)(2,1)S(1)}, bf16[4,256,256]{2,1,0:T(8,128)(2,1)}, u32[]{:S(2)}) copy-start(bf16[4,256,256]{2,1,0:T(8,128)(2,1)} %param.9) | copy-start | bytes 1572868
  1.0 7.8 %collective-permute-start.1 = (bf16[1,104,256]{2,1,0:T(8,128)(2,1)S(1)}, bf16[1,104,256]{2,1,0:T(8,128)(2,1)S(1)}, u32[]{:S(2)}, u32[]{:S(2)}) collective-permute-start(bf16[1,104,256]{2,1,0:T(8,128)(2,1)S(1)} %get-tuple-element.47), channel_id=1, source_target_pairs={{1,0},{2,1},{3,2},{4,3},{5,4},{6,5},{7,6},{9,8},{10,9},{11,10},{12... | collective-permute-start | bytes 159752 | tf_op jit(solution)/shard_map/ppermute | solution.py:23
  2.3 6.9 %collective-permute-start = (bf16[1,104,256]{2,1,0:T(8,128)(2,1)S(1)}, bf16[1,104,256]{2,1,0:T(8,128)(2,1)S(1)}, u32[]{:S(2)}, u32[]{:S(2)}) collective-permute-start(bf16[1,104,256]{2,1,0:T(8,128)(2,1)S(1)} %get-tuple-element.46), channel_id=1, source_target_pairs={{0,1},{1,2},{2,3},{3,4},{4,5},{5,6},{6,7},{8,9},{9,10},{10,11},{11... | collective-permute-start | bytes 159752 | tf_op jit(solution)/shard_map/ppermute | solution.py:21
  9.2 1.1 copy-start.7
  146.8 2.4 copy-start.8
  149.1 1.8 copy-start.1
  156.4 63.3 %all-to-all-start = ((bf16[32,8,13,768]{3,0,2,1:T(8,128)(2,1)}), bf16[32,8,13,768]{3,0,2,1:T(8,128)(2,1)}, u32[]{:S(2)}, u32[]{:S(2)}) async-start(bf16[32,8,13,768]{3,0,2,1:T(8,128)(2,1)} %bitcast.103), calls=%async_computation | async-start | bytes 10223616 | tf_op jit(solution)/shard_map/all_to_all | solution.py:109
  222.7 2.3 copy-start.3
  294.1 0.9 copy-start.6
  294.7 2.0 copy-start.2
where the time goes:
time: 301 us; the launch traced here: 300 us
  blocking collectives  164 us (54%)
  waiting for transfers between devices  58.5 us (19%)
  local copies, waits for them, and re-layouts  33.9 us (11%)
  matrix products  27.1 us (9%)
  starting transfers between devices  10.6 us (4%)
  other arithmetic  5.31 us (2%)
    psum x1, blocking collectives, normalize(): lax.psum(by_group(jnp.sum(upsampled_float, axis=(0, 1))), ('rows', 'frame...  71.1 us
    psum x1, blocking collectives, normalize(): lax.psum(by_group(jnp.sum(centered * centered, axis=(0, 1))), ('rows', 'f...  62.3 us
    all_to_all x1, waiting for transfers between devices, per_device(): lax.all_to_all(projected.reshape(out_local, frame_devices, pixel_share, 3...  58.5 us
    all_to_all x1, blocking collectives, per_device(): lax.all_to_all(shortened(context), 'frames', split_axis=0, concat_axis=1,...  30.8 us
    sub x4, matrix products, attend_pixel(): scores = scores - jnp.max(scores, axis=-1, keepdims=True)  10.9 us
    dot_general x4, matrix products, attend_pixel(): jnp.einsum('hqk,khd->qhd', probabilities, values, preferred_element_type=...  8.4 us
    dynamic_slice x6, local copies, waits for them, and re-layouts, per_device(): context = lax.map(attend_pixel, per_pixel, batch_size=4)  6.62 us
  transfers between devices with their start and end apart: 3, of which 1 were waited for; matrix products, arithmetic and copies ran while one was open for 1% of the time, Pallas kernels for 0%

commit v1 on v0

v1 whole, which is shorter than its diff:
```python
import functools

import jax
import jax.numpy as jnp
from jax import lax
from jax.experimental import pallas as pl
from jax.experimental.pallas import tpu as pltpu
from jax.sharding import PartitionSpec as P

HEAD_DIM = 64
GROUPS = 32
EPSILON = 1e-06
LANES = 128
LOG2E = 1.4426950408889634
HIGHEST = lax.Precision.HIGHEST
BF16 = jnp.bfloat16
F32 = jnp.float32
NT = (((1,), (1,)), ((), ()))


def params(mib):
    return pltpu.CompilerParams(vmem_limit_bytes=mib * 1024 * 1024)


def pack_kernel(latent_ref, embed_ref, out_ref, wide, embed_wide):
    frames, pixels, _ = latent_ref.shape
    devices = out_ref.shape[0]
    share = pixels // devices
    for half in range(wide.shape[0]):
        lanes = slice(half * LANES, (half + 1) * LANES)
        for f in range(frames):
            wide[half, f * pixels : (f + 1) * pixels, :] = latent_ref[f, :, lanes].astype(F32)
        embed_wide[half] = embed_ref[:, lanes].astype(F32)
        for p in range(pixels):
            d, j = divmod(p, share)
            rows = wide[half, pl.ds(p, frames, stride=pixels), :].astype(BF16)
            out_ref[d, j * frames : (j + 1) * frames, lanes] = rows
        for parity in range(2):
            rows = embed_wide[half, pl.ds(parity, frames, stride=2), :].astype(BF16)
            base = share * frames + parity * frames
            for d in range(devices):
                out_ref[d, base : base + frames, lanes] = rows


def pack(latent, frame_embed, devices):
    frames, pixels, channels = latent.shape
    rows = pixels // devices * frames + 2 * frames
    return pl.pallas_call(
        pack_kernel,
        out_shape=jax.ShapeDtypeStruct((devices, rows, channels), BF16),
        scratch_shapes=[
            pltpu.VMEM((channels // LANES, frames * pixels, LANES), F32),
            pltpu.VMEM((channels // LANES, 2 * frames, LANES), F32),
        ],
        compiler_params=params(24),
        name="pack_latent",
    )(latent, frame_embed)


def group_matrix(channels, offset):
    size = channels // GROUPS
    channel = lax.broadcasted_iota(jnp.int32, (channels, LANES), 0)
    lane = lax.broadcasted_iota(jnp.int32, (channels, LANES), 1)
    return jnp.where(channel // size + offset == lane, 1.0, 0.0).astype(F32)


def group_spread(channels):
    size = channels // GROUPS
    lane = lax.broadcasted_iota(jnp.int32, (LANES, channels), 0)
    channel = lax.broadcasted_iota(jnp.int32, (LANES, channels), 1)
    return jnp.where(channel // size == lane, 1.0, 0.0).astype(F32)


def exact_dot(a, b):
    return jnp.dot(a, b, precision=HIGHEST, preferred_element_type=F32)


def upsample_kernel(share, block_ref, conv_ref, up_ref, stats_ref, taps):
    devices = block_ref.shape[0]
    channels = block_ref.shape[2]
    part = (block_ref.shape[1]) // (share + 2)
    length = devices * part
    row = lax.broadcasted_iota(jnp.int32, (length, channels), 0)
    for j in range(share):
        here = jnp.concatenate([block_ref[s, j * part : (j + 1) * part, :] for s in range(devices)], axis=0)
        wide = here.astype(F32)
        before = jnp.where(row == 0, 0.0, pltpu.roll(wide, 1, 0))
        after = jnp.where(row == length - 1, 0.0, pltpu.roll(wide, length - 1, 0))
        rows = slice(j * length, (j + 1) * length)
        taps[0, rows, :] = before.astype(BF16)
        taps[1, rows, :] = here
        taps[2, rows, :] = after.astype(BF16)

    def tap(source, index):
        return jnp.dot(taps[source], conv_ref[index], preferred_element_type=F32)

    even = (tap(1, 1) + tap(0, 3)).astype(BF16)
    odd = (tap(2, 0) + tap(1, 2)).astype(BF16)
    for j in range(share):
        up_ref[j, 0] = even[j * length : (j + 1) * length]
        up_ref[j, 1] = odd[j * length : (j + 1) * length]
    count = share * 2 * length * (channels // GROUPS)
    total = jnp.zeros((8, channels), F32)

    def add_rows(i, total):
        chunk = up_ref[i].astype(F32).reshape(-1, 8, channels)
        return total + jnp.sum(chunk, axis=0)

    total = lax.fori_loop(0, share, add_rows, total)
    total = jnp.broadcast_to(jnp.sum(total, axis=0, keepdims=True), (8, channels))
    mean = exact_dot(total, group_matrix(channels, 0)) / count
    center = exact_dot(mean, group_spread(channels))[0:1]

    def add_squares(i, spread):
        away = (up_ref[i].astype(F32).reshape(-1, channels) - center).reshape(-1, 8, channels)
        return spread + jnp.sum(away * away, axis=0)

    spread = lax.fori_loop(0, share, add_squares, jnp.zeros((8, channels), F32))
    spread = jnp.broadcast_to(jnp.sum(spread, axis=0, keepdims=True), (8, channels))
    stats_ref[...] = (mean + exact_dot(spread, group_matrix(channels, LANES // 2)))[0:1]


def upsample(block, conv_weight, share):
    devices, rows, channels = block.shape
    length = devices * (rows // (share + 2))
    return pl.pallas_call(
        functools.partial(upsample_kernel, share),
        out_shape=(
            jax.ShapeDtypeStruct((share, 2, length, channels), BF16),
            jax.ShapeDtypeStruct((1, LANES), F32),
        ),
        scratch_shapes=[pltpu.VMEM((3, share * length, channels), BF16)],
        compiler_params=params(48),
        name="upsample",
    )(block, conv_weight)


def attend_kernel(
    count, up_ref, stats_ref, gain_ref, block_ref, qkv_ref, out_weight_ref, out_ref, embed, wq_t, wv_t
):
    share, _, length, channels = up_ref.shape
    devices = block_ref.shape[0]
    part = length // devices
    frames = 2 * length
    heads = channels // HEAD_DIM
    per_lane = LANES // HEAD_DIM

    stats = stats_ref[...].reshape(-1, LANES)
    holders = stats.shape[0]
    center = jnp.sum(stats, axis=0, keepdims=True) / holders
    away = stats - center
    between = jnp.sum(away * away, axis=0, keepdims=True) * count
    within = pltpu.roll(center, LANES // 2, 1) * holders
    lane = lax.broadcasted_iota(jnp.int32, (1, LANES), 1)
    variance = jnp.where(lane < GROUPS, (between + within) / (count * holders), 0.0)
    center = jnp.where(lane < GROUPS, center, 0.0)
    moments = jnp.concatenate(
        [jnp.broadcast_to(center, (8, LANES)), jnp.broadcast_to(variance, (8, LANES))], axis=0
    )
    moments = exact_dot(moments, group_spread(channels))
    center = moments[0:1]
    scale = lax.rsqrt(moments[8:9] + EPSILON) * gain_ref[...].astype(F32)

    base = share * part
    for parity in range(2):
        for s in range(devices):
            start = base + parity * part
            embed[parity * length + s * part : parity * length + (s + 1) * part, :] = block_ref[
                s, start : start + part, :
            ].astype(F32)
    wq_t[...] = qkv_ref[:, 0:channels].astype(F32).T.astype(BF16)
    wv_t[...] = qkv_ref[:, 2 * channels : 3 * channels].astype(F32).T.astype(BF16)
    empty = jnp.zeros((HEAD_DIM, frames), BF16)

    def one_pixel(j, carry):
        up = up_ref[j].reshape(frames, channels).astype(F32)
        normed = ((up - center) * scale + embed[...]).astype(BF16)
        keys = jnp.dot(normed, qkv_ref[:, channels : 2 * channels], preferred_element_type=F32).astype(BF16)
        queries_t = lax.dot_general(wq_t[...], normed, NT, preferred_element_type=F32).astype(BF16)
        values_t = lax.dot_general(wv_t[...], normed, NT, preferred_element_type=F32).astype(BF16)
        context_t = []
        for h in range(heads):
            pair, place = divmod(h, per_lane)
            query = queries_t[h * HEAD_DIM : (h + 1) * HEAD_DIM, :]
            query = jnp.concatenate([query if i == place else empty for i in range(per_lane)], axis=0)
            scores = jnp.dot(keys[:, pair * LANES : (pair + 1) * LANES], query, preferred_element_type=F32)
            top = jnp.max(scores, axis=0, keepdims=True)
            weights = jnp.exp2((scores - top) * (LOG2E * HEAD_DIM**-0.5))
            total = jnp.sum(weights, axis=0, keepdims=True)
            probabilities = (weights * (1.0 / total)).astype(BF16)
            context_t.append(
                jnp.dot(
                    values_t[h * HEAD_DIM : (h + 1) * HEAD_DIM, :], probabilities, preferred_element_type=F32
                )
            )
        context = jnp.concatenate(context_t, axis=0).T.astype(BF16)
        mixed = jnp.dot(context, out_weight_ref[...], preferred_element_type=F32)
        blended = (up + mixed).astype(BF16)
        for d in range(devices):
            for parity in range(2):
                out_ref[d, j, parity] = blended[parity * length + d * part : parity * length + (d + 1) * part]
        return carry

    lax.fori_loop(0, share, one_pixel, 0)


def attend(up, stats, norm_gain, block, qkv_weight, out_weight):
    share, _, length, channels = up.shape
    devices = block.shape[0]
    part = length // devices
    count = share * 2 * length * (channels // GROUPS)
    return pl.pallas_call(
        functools.partial(attend_kernel, count),
        out_shape=jax.ShapeDtypeStruct((devices, share, 2, part, channels), BF16),
        scratch_shapes=[
            pltpu.VMEM((2 * length, channels), F32),
            pltpu.VMEM((channels, channels), BF16),
            pltpu.VMEM((channels, channels), BF16),
        ],
        compiler_params=params(48),
        name="attend",
    )(up, stats, norm_gain.reshape(1, channels), block, qkv_weight, out_weight)


def unpack_kernel(block_ref, out_ref, wide):
    devices, share, _, part, _ = block_ref.shape
    frames, pixels, _ = out_ref.shape
    for half in range(wide.shape[0]):
        lanes = slice(half * LANES, (half + 1) * LANES)
        for s in range(devices):
            for j in range(share):
                for parity in range(2):
                    start = parity * pixels + s * share + j
                    rows = block_ref[s, j, parity, :, lanes].astype(F32)
                    wide[half, pl.ds(start, part, stride=2 * pixels), :] = rows
        for f in range(frames):
            out_ref[f, :, lanes] = wide[half, f * pixels : (f + 1) * pixels, :].astype(BF16)


def unpack(block):
    devices, share, _, part, channels = block.shape
    frames, pixels = 2 * part, devices * share
    return pl.pallas_call(
        unpack_kernel,
        out_shape=jax.ShapeDtypeStruct((frames, pixels, channels), BF16),
        scratch_shapes=[pltpu.VMEM((channels // LANES, frames * pixels, LANES), F32)],
        compiler_params=params(24),
        name="unpack_output",
    )(block)


def per_device(latent, conv_weight, norm_gain, frame_embed, qkv_weight, out_weight):
    devices = lax.axis_size("frames")
    everyone = devices * lax.axis_size("rows")
    share = latent.shape[1] // devices
    sent = pack(latent, frame_embed, devices)
    block = lax.all_to_all(sent, "frames", 0, 0)
    up, stats = upsample(block, conv_weight, share)
    stats = lax.all_to_all(
        jnp.broadcast_to(stats[None], (everyone,) + stats.shape), ("rows", "frames"), 0, 0
    )
    blended = attend(up, stats, norm_gain, block, qkv_weight, out_weight)
    return unpack(lax.all_to_all(blended, "frames", 0, 0))


def solution(mesh):
    return jax.shard_map(
        per_device,
        mesh=mesh,
        in_specs=(P("frames", "rows", None), P(), P(), P("frames", None), P(), P()),
        out_specs=P("frames", "rows", None),
        check_vma=False,
    )
```

time: 301 us -> 96 us (0.32)
  blocking collectives: 164 us -> 47 us
  waiting for transfers between devices: 58.5 us -> 9.21 us
  local copies, waits for them, and re-layouts: 33.9 us -> 2.59 us
  Pallas kernels: 0 us -> 29.2 us
  matrix products: 27.1 us -> 0 us
  other arithmetic: 5.31 us -> 0 us
    psum x2 -> x0, blocking collectives: 133 us -> none  [the longest x1 71.1 us: normalize(): lax.psum(by_group(jnp.sum(upsampled_float, axis=(0, 1))), ('rows', 'frame...]
    all_to_all x1, waiting for transfers between devices: 58.5 us -> 9.21 us  [per_device(): lax.all_to_all(jnp.broadcast_to(stats[None], (everyone,) + stats.shape),...]
    pallas_call x0 -> x4, Pallas kernels: none -> 29.2 us  [the longest x1 23.7 us: attend(): pl.pallas_call(functools.partial(attend_kernel, count), out_shape=jax.Sha...]
    all_to_all x1 -> x2, blocking collectives: 30.8 us -> 47 us  [the longest x1 25.6 us: per_device(): return unpack(lax.all_to_all(blended, 'frames', 0, 0))]
    dot_general x11 -> x0, matrix products: 16.2 us -> none  [the longest x4 8.4 us: attend_pixel(): jnp.einsum('hqk,khd->qhd', probabilities, values, preferred_element_type=...]
    sub x4 -> x0, matrix products: 10.9 us -> none  [attend_pixel(): scores = scores - jnp.max(scores, axis=-1, keepdims=True)]
    dynamic_slice x6 -> x0, local copies, waits for them, and re-layouts: 6.62 us -> none  [per_device(): context = lax.map(attend_pixel, per_pixel, batch_size=4)]
    convert_element_type x3 -> x0, local copies, waits for them, and re-layouts: 6.57 us -> none  [the longest x1 3.46 us: per_device(): projected = jnp.einsum('fpc,cd->fpd', normed, qkv_weight, preferred_eleme...]
  transfers between devices with their start and end apart: 3 -> 1, of which waited for: 1 -> 1; matrix products, arithmetic and copies ran while one was open for 1% -> 0% of each run, Pallas kernels for 0% -> 0%
where the time goes in v1:
time: 96 us; the launch traced here: 95.7 us
  blocking collectives  47 us (49%)
  Pallas kernels  29.2 us (30%)
  waiting for transfers between devices  9.21 us (10%)
  starting transfers between devices  7.66 us (8%)
  local copies, waits for them, and re-layouts  2.59 us (3%)
    all_to_all x1, blocking collectives, per_device(): return unpack(lax.all_to_all(blended, 'frames', 0, 0))  25.6 us
    pallas_call x1, Pallas kernels, attend(): pl.pallas_call(functools.partial(attend_kernel, count), out_shape=jax.Sha...  23.7 us
    all_to_all x1, blocking collectives, per_device(): block = lax.all_to_all(sent, 'frames', 0, 0)  21.4 us
    all_to_all x1, waiting for transfers between devices, per_device(): lax.all_to_all(jnp.broadcast_to(stats[None], (everyone,) + stats.shape),...  9.21 us
    all_to_all x1, starting transfers between devices, per_device(): lax.all_to_all(jnp.broadcast_to(stats[None], (everyone,) + stats.shape),...  7.66 us
    pallas_call x1, Pallas kernels, upsample(): pl.pallas_call(functools.partial(upsample_kernel, share), out_shape=(jax....  2.67 us
    pallas_call x1, Pallas kernels, unpack(): pl.pallas_call(unpack_kernel, out_shape=jax.ShapeDtypeStruct((frames, pix...  2.4 us
  transfers between devices with their start and end apart: 1, of which 1 were waited for; matrix products, arithmetic and copies ran while one was open for 0% of the time, Pallas kernels for 0%

profile of v1, /device:TPU:0, one launch (start us, length us, event | category | flops | bytes accessed | tf_op | source)
XLA Modules:
  0.0 95.7 jit_solution(15807685349081659719)
XLA Ops:
  0.0 0.0 copy-start
  0.0 1.2 %copy-done = bf16[16,104,256]{2,1,0:T(8,128)(2,1)S(1)} copy-done((bf16[16,104,256]{2,1,0:T(8,128)(2,1)S(1)}, bf16[16,104,256]{2,1,0:T(8,128)(2,1)}, u32[]{:S(2)}) %copy-start) | copy-done | bytes 851992
  1.2 0.0 copy-start.4
  1.2 0.7 copy-done.4
  1.9 0.0 copy-start.1
  1.9 0.4 pack_latent.1
  2.3 0.0 copy-start.5
  2.3 0.0 copy-start.2
  2.3 0.0 copy-start.3
  2.4 21.4 %all_to_all.15.block_ref = bf16[8,240,256]{2,1,0:T(8,128)(2,1)S(1)} all-to-all(bf16[8,240,256]{2,1,0:T(8,128)(2,1)S(1)} %pack_latent.1), channel_id=1, replica_groups=mesh['rows'=16,'frames'=8] {'frames'}, dimensions={0} | all-to-all | bytes 1966080 | tf_op jit(solution)/shard_map/all_to_all | solution.py:257
  23.8 0.0 copy-done.1
  23.8 2.7 %upsample.1 = (bf16[13,2,128,256]{3,2,1,0:T(8,128)(2,1)S(1)}, f32[1,128]{1,0:T(1,128)S(1)}) custom-call(bf16[8,240,256]{2,1,0:T(8,128)(2,1)S(1)} %all_to_all.15.block_ref, bf16[4,256,256]{2,1,0:T(8,128)(2,1)S(1)} %copy-done.1), custom_call_target="tpu_custom_call" | custom-call | tf_op jit(solution)/shard_map/upsample/pallas_call | solution.py:126
  26.5 0.7 broadcast_in_dim.9
  27.1 7.7 %all-to-all-start.1 = ((f32[128,1,128]{2,1,0:T(1,128)}), f32[128,1,128]{2,1,0:T(1,128)S(1)}, u32[]{:S(2)}, u32[]{:S(2)}) async-start(f32[128,1,128]{2,1,0:T(1,128)} %broadcast_in_dim.9), calls=%async_computation.1 | async-start | bytes 131072 | tf_op jit(solution)/shard_map/all_to_all | solution.py:259
  34.8 0.0 copy-done.5
  34.8 9.2 %all-to-all-done.1.stats_ref = f32[128,1,128]{2,1,0:T(1,128)S(1)} async-done(((f32[128,1,128]{2,1,0:T(1,128)}), f32[128,1,128]{2,1,0:T(1,128)S(1)}, u32[]{:S(2)}, u32[]{:S(2)}) %all-to-all-start.1) | async-done | bytes 65568 | tf_op jit(solution)/shard_map/all_to_all | solution.py:259
  44.1 0.0 copy-done.2
  44.1 0.0 copy-done.3
  44.1 23.7 %attend.1 = bf16[8,13,2,16,256]{4,3,2,1,0:T(8,128)(2,1)S(1)} custom-call(bf16[13,2,128,256]{3,2,1,0:T(8,128)(2,1)S(1)} %get-tuple-element.7.up_ref, f32[128,1,128]{2,1,0:T(1,128)S(1)} %all-to-all-done.1.stats_ref, bf16[1,256]{1,0:T(2,128)(2,1)S(1)} %reshape.6.gain_ref, bf16[8,240,256]{2,1,0:T(8,128)(2,1)S(1)} %all_to_all.15.block_ref, ...), custom_call_target="tpu_custom_call" | custom-call | tf_op jit(solution)/shard_map/attend/pallas_call | solution.py:212
  67.7 25.6 %all_to_all.16.block_ref = bf16[8,13,2,16,256]{4,3,2,1,0:T(8,128)(2,1)S(1)} all-to-all(bf16[8,13,2,16,256]{4,3,2,1,0:T(8,128)(2,1)S(1)} %attend.1), channel_id=1, replica_groups=mesh['rows'=16,'frames'=8] {'frames'}, dimensions={0} | all-to-all | bytes 3407872 | tf_op jit(solution)/shard_map/all_to_all | solution.py:263
  93.3 2.4 %unpack_output.1 = bf16[32,104,256]{2,1,0:T(8,128)(2,1)} custom-call(bf16[8,13,2,16,256]{4,3,2,1,0:T(8,128)(2,1)S(1)} %all_to_all.16.block_ref), custom_call_target="tpu_custom_call" | custom-call | tf_op jit(solution)/shard_map/unpack_output/pallas_call | solution.py:243
  (1 shorter events, 0.0 us)
Async XLA Ops:
  0.0 1.2 %copy-start = (bf16[16,104,256]{2,1,0:T(8,128)(2,1)S(1)}, bf16[16,104,256]{2,1,0:T(8,128)(2,1)}, u32[]{:S(2)}) copy-start(bf16[16,104,256]{2,1,0:T(8,128)(2,1)} %latent_ref.1) | copy-start | bytes 2555908
  1.2 0.7 copy-start.4
  1.9 21.9 %copy-start.1 = (bf16[4,256,256]{2,1,0:T(8,128)(2,1)S(1)}, bf16[4,256,256]{2,1,0:T(8,128)(2,1)}, u32[]{:S(2)}) copy-start(bf16[4,256,256]{2,1,0:T(8,128)(2,1)} %conv_ref.1) | copy-start | bytes 1572868
  2.3 32.5 %copy-start.5 = (bf16[256]{0:T(256)(128)(2,1)S(1)}, bf16[256]{0:T(256)(128)(2,1)}, u32[]{:S(2)}) copy-start(bf16[256]{0:T(256)(128)(2,1)} %param.8) | copy-start | bytes 1540
  2.3 41.7 %copy-start.2 = (bf16[256,768]{1,0:T(8,128)(2,1)S(1)}, bf16[256,768]{1,0:T(8,128)(2,1)}, u32[]{:S(2)}) copy-start(bf16[256,768]{1,0:T(8,128)(2,1)} %qkv_ref.1) | copy-start | bytes 1179652
  2.3 41.7 %copy-start.3 = (bf16[256,256]{1,0:T(8,128)(2,1)S(1)}, bf16[256,256]{1,0:T(8,128)(2,1)}, u32[]{:S(2)}) copy-start(bf16[256,256]{1,0:T(8,128)(2,1)} %out_weight_ref.1) | copy-start | bytes 393220
  27.1 16.9 %all-to-all-start.1 = ((f32[128,1,128]{2,1,0:T(1,128)}), f32[128,1,128]{2,1,0:T(1,128)S(1)}, u32[]{:S(2)}, u32[]{:S(2)}) async-start(f32[128,1,128]{2,1,0:T(1,128)} %broadcast_in_dim.9), calls=%async_computation.1 | async-start | bytes 131072 | tf_op jit(solution)/shard_map/all_to_all | solution.py:259

commit v2 on v1

--- a/solution.py
+++ b/solution.py
@@ -135,17 +135,8 @@
     )(block, conv_weight)
 
 
-def attend_kernel(
-    count, up_ref, stats_ref, gain_ref, block_ref, qkv_ref, out_weight_ref, out_ref, embed, wq_t, wv_t
-):
-    share, _, length, channels = up_ref.shape
-    devices = block_ref.shape[0]
-    part = length // devices
-    frames = 2 * length
-    heads = channels // HEAD_DIM
-    per_lane = LANES // HEAD_DIM
-
-    stats = stats_ref[...].reshape(-1, LANES)
+def moments(stats, count, gain):
+    channels = gain.shape[1]
     holders = stats.shape[0]
     center = jnp.sum(stats, axis=0, keepdims=True) / holders
     away = stats - center
@@ -154,13 +145,46 @@
     lane = lax.broadcasted_iota(jnp.int32, (1, LANES), 1)
     variance = jnp.where(lane < GROUPS, (between + within) / (count * holders), 0.0)
     center = jnp.where(lane < GROUPS, center, 0.0)
-    moments = jnp.concatenate(
+    both = jnp.concatenate(
         [jnp.broadcast_to(center, (8, LANES)), jnp.broadcast_to(variance, (8, LANES))], axis=0
     )
-    moments = exact_dot(moments, group_spread(channels))
-    center = moments[0:1]
-    scale = lax.rsqrt(moments[8:9] + EPSILON) * gain_ref[...].astype(F32)
-
+    both = exact_dot(both, group_spread(channels))
+    return both[0:1], lax.rsqrt(both[8:9] + EPSILON) * gain.astype(F32)
+
+
+def attend_pixel(qkv):
+    rows, channels = qkv.shape[0], qkv.shape[1] // 3
+    heads = channels // HEAD_DIM
+    head = lax.broadcasted_iota(jnp.int32, (rows, channels), 1) // HEAD_DIM
+    first = lax.broadcasted_iota(jnp.int32, (rows, LANES), 1) < HEAD_DIM
+    queries, keys, values = (qkv[:, i * channels : (i + 1) * channels] for i in range(3))
+    zeros = jnp.zeros_like(queries)
+    stacked = jnp.concatenate([jnp.where(head == h, queries, zeros) for h in range(heads)], axis=0)
+    scores = lax.dot_general(stacked, keys, NT, preferred_element_type=F32)
+    ones = jnp.ones((rows, LANES), BF16)
+    context = []
+    for pair in range(heads // 2):
+        part = scores[pair * 2 * rows : (pair + 1) * 2 * rows]
+        top = jnp.max(part, axis=1, keepdims=True)
+        weights = jnp.exp2((part - top) * (LOG2E * HEAD_DIM**-0.5)).astype(BF16)
+        value = jnp.concatenate([values[:, pair * LANES : (pair + 1) * LANES], ones], axis=1)
+        sums = jnp.dot(weights, value, preferred_element_type=F32)
+        above, total = (
+            jnp.where(first, sums[:rows, i * LANES : (i + 1) * LANES], sums[rows:, i * LANES : (i + 1) * LANES])
+            for i in range(2)
+        )
+        context.append((above * (1.0 / total)).astype(BF16))
+    return jnp.concatenate(context, axis=1)
+
+
+def attend_kernel(
+    count, batch, up_ref, stats_ref, gain_ref, block_ref, qkv_ref, out_weight_ref, out_ref, embed, projected, context
+):
+    share, _, length, channels = up_ref.shape
+    devices = block_ref.shape[0]
+    part = length // devices
+    frames = 2 * length
+    center, scale = moments(stats_ref[...].reshape(-1, LANES), count, gain_ref[...])
     base = share * part
     for parity in range(2):
         for s in range(devices):
@@ -168,40 +192,31 @@
             embed[parity * length + s * part : parity * length + (s + 1) * part, :] = block_ref[
                 s, start : start + part, :
             ].astype(F32)
-    wq_t[...] = qkv_ref[:, 0:channels].astype(F32).T.astype(BF16)
-    wv_t[...] = qkv_ref[:, 2 * channels : 3 * channels].astype(F32).T.astype(BF16)
-    empty = jnp.zeros((HEAD_DIM, frames), BF16)
-
-    def one_pixel(j, carry):
+
+    def project(first, pixels):
+        up = up_ref[pl.ds(first, pixels)].reshape(pixels, frames, channels).astype(F32)
+        normed = ((up - center) * scale + embed[...]).astype(BF16).reshape(pixels * frames, channels)
+        rows = pl.ds(pl.multiple_of(first * frames, frames), pixels * frames)
+        projected[rows, :] = jnp.dot(normed, qkv_ref[...], preferred_element_type=F32).astype(BF16)
+
+    def project_batch(i, carry):
+        project(i * batch, batch)
+        return carry
+
+    lax.fori_loop(0, share // batch, project_batch, 0)
+    if share % batch:
+        project(share - share % batch, share % batch)
+    for j in range(share):
+        rows = slice(j * frames, (j + 1) * frames)
+        context[rows, :] = attend_pixel(projected[rows, :])
+    mixed = jnp.dot(context[...], out_weight_ref[...], preferred_element_type=F32)
+    for j in range(share):
         up = up_ref[j].reshape(frames, channels).astype(F32)
-        normed = ((up - center) * scale + embed[...]).astype(BF16)
-        keys = jnp.dot(normed, qkv_ref[:, channels : 2 * channels], preferred_element_type=F32).astype(BF16)
-        queries_t = lax.dot_general(wq_t[...], normed, NT, preferred_element_type=F32).astype(BF16)
-        values_t = lax.dot_general(wv_t[...], normed, NT, preferred_element_type=F32).astype(BF16)
-        context_t = []
-        for h in range(heads):
-            pair, place = divmod(h, per_lane)
-            query = queries_t[h * HEAD_DIM : (h + 1) * HEAD_DIM, :]
-            query = jnp.concatenate([query if i == place else empty for i in range(per_lane)], axis=0)
-            scores = jnp.dot(keys[:, pair * LANES : (pair + 1) * LANES], query, preferred_element_type=F32)
-            top = jnp.max(scores, axis=0, keepdims=True)
-            weights = jnp.exp2((scores - top) * (LOG2E * HEAD_DIM**-0.5))
-            total = jnp.sum(weights, axis=0, keepdims=True)
-            probabilities = (weights * (1.0 / total)).astype(BF16)
-            context_t.append(
-                jnp.dot(
-                    values_t[h * HEAD_DIM : (h + 1) * HEAD_DIM, :], probabilities, preferred_element_type=F32
-                )
-            )
-        context = jnp.concatenate(context_t, axis=0).T.astype(BF16)
-        mixed = jnp.dot(context, out_weight_ref[...], preferred_element_type=F32)
-        blended = (up + mixed).astype(BF16)
+        blended = (up + mixed[j * frames : (j + 1) * frames]).astype(BF16)
         for d in range(devices):
             for parity in range(2):
-                out_ref[d, j, parity] = blended[parity * length + d * part : parity * length + (d + 1) * part]
-        return carry
-
-    lax.fori_loop(0, share, one_pixel, 0)
+                start = parity * length + d * part
+                out_ref[d, j, parity] = blended[start : start + part]
 
 
 def attend(up, stats, norm_gain, block, qkv_weight, out_weight):
@@ -209,13 +224,14 @@
     devices = block.shape[0]
     part = length // devices
     count = share * 2 * length * (channels // GROUPS)
-    return pl.pallas_call(
-        functools.partial(attend_kernel, count),
+    rows = share * 2 * length
+    return pl.pallas_call(
+        functools.partial(attend_kernel, count, 4),
         out_shape=jax.ShapeDtypeStruct((devices, share, 2, part, channels), BF16),
         scratch_shapes=[
             pltpu.VMEM((2 * length, channels), F32),
-            pltpu.VMEM((channels, channels), BF16),
-            pltpu.VMEM((channels, channels), BF16),
+            pltpu.VMEM((rows, 3 * channels), BF16),
+            pltpu.VMEM((rows, channels), BF16),
         ],
         compiler_params=params(48),
         name="attend",

time: 96 us -> 78.8 us (0.82)
  Pallas kernels: 29.2 us -> 12 us
    pallas_call x1, Pallas kernels: 23.7 us -> 6.47 us  [attend(): pl.pallas_call(functools.partial(attend_kernel, count, 4), out_shape=jax....]
where the time goes in v2:
time: 78.8 us; the launch traced here: 78.5 us
  blocking collectives  47 us (60%)
  Pallas kernels  12 us (15%)
  waiting for transfers between devices  9.21 us (12%)
  starting transfers between devices  7.66 us (10%)
  local copies, waits for them, and re-layouts  2.59 us (3%)
    all_to_all x1, blocking collectives, per_device(): return unpack(lax.all_to_all(blended, 'frames', 0, 0))  25.6 us
    all_to_all x1, blocking collectives, per_device(): block = lax.all_to_all(sent, 'frames', 0, 0)  21.4 us
    all_to_all x1, waiting for transfers between devices, per_device(): lax.all_to_all(jnp.broadcast_to(stats[None], (everyone,) + stats.shape),...  9.21 us
    all_to_all x1, starting transfers between devices, per_device(): lax.all_to_all(jnp.broadcast_to(stats[None], (everyone,) + stats.shape),...  7.66 us
    pallas_call x1, Pallas kernels, attend(): pl.pallas_call(functools.partial(attend_kernel, count, 4), out_shape=jax....  6.47 us
    pallas_call x1, Pallas kernels, upsample(): pl.pallas_call(functools.partial(upsample_kernel, share), out_shape=(jax....  2.67 us
    pallas_call x1, Pallas kernels, unpack(): pl.pallas_call(unpack_kernel, out_shape=jax.ShapeDtypeStruct((frames, pix...  2.4 us
    unnamed x12, local copies, waits for them, and re-layouts  1.89 us
  transfers between devices with their start and end apart: 1, of which 1 were waited for; matrix products, arithmetic and copies ran while one was open for 0% of the time, Pallas kernels for 0%

profile of v2, /device:TPU:0, one launch (start us, length us, event | category | flops | bytes accessed | tf_op | source)
XLA Modules:
  0.0 78.5 jit_solution(9211314614928446032)
XLA Ops:
  0.0 0.0 copy-start
  0.0 1.2 %copy-done = bf16[16,104,256]{2,1,0:T(8,128)(2,1)S(1)} copy-done((bf16[16,104,256]{2,1,0:T(8,128)(2,1)S(1)}, bf16[16,104,256]{2,1,0:T(8,128)(2,1)}, u32[]{:S(2)}) %copy-start) | copy-done | bytes 851992
  1.2 0.0 copy-start.4
  1.2 0.7 copy-done.4
  1.9 0.0 copy-start.1
  1.9 0.4 pack_latent.1
  2.3 0.0 copy-start.5
  2.3 0.0 copy-start.2
  2.3 0.0 copy-start.3
  2.4 21.4 %all_to_all.15.block_ref = bf16[8,240,256]{2,1,0:T(8,128)(2,1)S(1)} all-to-all(bf16[8,240,256]{2,1,0:T(8,128)(2,1)S(1)} %pack_latent.1), channel_id=1, replica_groups=mesh['rows'=16,'frames'=8] {'frames'}, dimensions={0} | all-to-all | bytes 1966080 | tf_op jit(solution)/shard_map/all_to_all | solution.py:273
  23.8 0.0 copy-done.1
  23.8 2.7 %upsample.1 = (bf16[13,2,128,256]{3,2,1,0:T(8,128)(2,1)S(1)}, f32[1,128]{1,0:T(1,128)S(1)}) custom-call(bf16[8,240,256]{2,1,0:T(8,128)(2,1)S(1)} %all_to_all.15.block_ref, bf16[4,256,256]{2,1,0:T(8,128)(2,1)S(1)} %copy-done.1), custom_call_target="tpu_custom_call" | custom-call | tf_op jit(solution)/shard_map/upsample/pallas_call | solution.py:126
  26.5 0.7 broadcast_in_dim.9
  27.1 7.7 %all-to-all-start.1 = ((f32[128,1,128]{2,1,0:T(1,128)}), f32[128,1,128]{2,1,0:T(1,128)S(1)}, u32[]{:S(2)}, u32[]{:S(2)}) async-start(f32[128,1,128]{2,1,0:T(1,128)} %broadcast_in_dim.9), calls=%async_computation.1 | async-start | bytes 131072 | tf_op jit(solution)/shard_map/all_to_all | solution.py:275
  34.8 0.0 copy-done.5
  34.8 9.2 %all-to-all-done.1.stats_ref = f32[128,1,128]{2,1,0:T(1,128)S(1)} async-done(((f32[128,1,128]{2,1,0:T(1,128)}), f32[128,1,128]{2,1,0:T(1,128)S(1)}, u32[]{:S(2)}, u32[]{:S(2)}) %all-to-all-start.1) | async-done | bytes 65568 | tf_op jit(solution)/shard_map/all_to_all | solution.py:275
  44.1 0.0 copy-done.2
  44.1 0.0 copy-done.3
  44.1 6.5 %attend.1 = bf16[8,13,2,16,256]{4,3,2,1,0:T(8,128)(2,1)S(1)} custom-call(bf16[13,2,128,256]{3,2,1,0:T(8,128)(2,1)S(1)} %get-tuple-element.7.up_ref, f32[128,1,128]{2,1,0:T(1,128)S(1)} %all-to-all-done.1.stats_ref, bf16[1,256]{1,0:T(2,128)(2,1)S(1)} %reshape.6.gain_ref, bf16[8,240,256]{2,1,0:T(8,128)(2,1)S(1)} %all_to_all.15.block_ref, ...), custom_call_target="tpu_custom_call" | custom-call | tf_op jit(solution)/shard_map/attend/pallas_call | solution.py:228
  50.5 25.6 %all_to_all.16.block_ref = bf16[8,13,2,16,256]{4,3,2,1,0:T(8,128)(2,1)S(1)} all-to-all(bf16[8,13,2,16,256]{4,3,2,1,0:T(8,128)(2,1)S(1)} %attend.1), channel_id=1, replica_groups=mesh['rows'=16,'frames'=8] {'frames'}, dimensions={0} | all-to-all | bytes 3407872 | tf_op jit(solution)/shard_map/all_to_all | solution.py:279
  76.1 2.4 %unpack_output.1 = bf16[32,104,256]{2,1,0:T(8,128)(2,1)} custom-call(bf16[8,13,2,16,256]{4,3,2,1,0:T(8,128)(2,1)S(1)} %all_to_all.16.block_ref), custom_call_target="tpu_custom_call" | custom-call | tf_op jit(solution)/shard_map/unpack_output/pallas_call | solution.py:259
  (1 shorter events, 0.0 us)
Async XLA Ops:
  0.0 1.2 %copy-start = (bf16[16,104,256]{2,1,0:T(8,128)(2,1)S(1)}, bf16[16,104,256]{2,1,0:T(8,128)(2,1)}, u32[]{:S(2)}) copy-start(bf16[16,104,256]{2,1,0:T(8,128)(2,1)} %latent_ref.1) | copy-start | bytes 2555908
  1.2 0.7 copy-start.4
  1.9 21.9 %copy-start.1 = (bf16[4,256,256]{2,1,0:T(8,128)(2,1)S(1)}, bf16[4,256,256]{2,1,0:T(8,128)(2,1)}, u32[]{:S(2)}) copy-start(bf16[4,256,256]{2,1,0:T(8,128)(2,1)} %conv_ref.1) | copy-start | bytes 1572868
  2.3 32.5 %copy-start.5 = (bf16[256]{0:T(256)(128)(2,1)S(1)}, bf16[256]{0:T(256)(128)(2,1)}, u32[]{:S(2)}) copy-start(bf16[256]{0:T(256)(128)(2,1)} %param.8) | copy-start | bytes 1540
  2.3 41.7 %copy-start.2 = (bf16[256,768]{1,0:T(8,128)(2,1)S(1)}, bf16[256,768]{1,0:T(8,128)(2,1)}, u32[]{:S(2)}) copy-start(bf16[256,768]{1,0:T(8,128)(2,1)} %qkv_ref.1) | copy-start | bytes 1179652
  2.3 41.7 %copy-start.3 = (bf16[256,256]{1,0:T(8,128)(2,1)S(1)}, bf16[256,256]{1,0:T(8,128)(2,1)}, u32[]{:S(2)}) copy-start(bf16[256,256]{1,0:T(8,128)(2,1)} %out_weight_ref.1) | copy-start | bytes 393220
  27.1 16.9 %all-to-all-start.1 = ((f32[128,1,128]{2,1,0:T(1,128)}), f32[128,1,128]{2,1,0:T(1,128)S(1)}, u32[]{:S(2)}, u32[]{:S(2)}) async-start(f32[128,1,128]{2,1,0:T(1,128)} %broadcast_in_dim.9), calls=%async_computation.1 | async-start | bytes 131072 | tf_op jit(solution)/shard_map/all_to_all | solution.py:275

commit v3 on v2

--- a/solution.py
+++ b/solution.py
@@ -96,38 +96,40 @@
 
     even = (tap(1, 1) + tap(0, 3)).astype(BF16)
     odd = (tap(2, 0) + tap(1, 2)).astype(BF16)
+    count = share * 2 * length * (channels // GROUPS)
+    fold = 32
+
+    def column_sums(pieces):
+        total = sum(jnp.sum(piece.reshape(-1, fold, channels), axis=0) for piece in pieces)
+        return jnp.broadcast_to(jnp.sum(total, axis=0, keepdims=True), (8, channels))
+
+    pivot = column_sums([frames[0:length].astype(F32) for frames in (even, odd)])
+    pivot = exact_dot(pivot, group_matrix(channels, 0)) * (share / count)
+    center = exact_dot(pivot, group_spread(channels))[0:1]
+    shifts = jnp.zeros((fold, channels), F32)
+    squares = jnp.zeros((fold, channels), F32)
     for j in range(share):
-        up_ref[j, 0] = even[j * length : (j + 1) * length]
-        up_ref[j, 1] = odd[j * length : (j + 1) * length]
-    count = share * 2 * length * (channels // GROUPS)
-    total = jnp.zeros((8, channels), F32)
-
-    def add_rows(i, total):
-        chunk = up_ref[i].astype(F32).reshape(-1, 8, channels)
-        return total + jnp.sum(chunk, axis=0)
-
-    total = lax.fori_loop(0, share, add_rows, total)
-    total = jnp.broadcast_to(jnp.sum(total, axis=0, keepdims=True), (8, channels))
-    mean = exact_dot(total, group_matrix(channels, 0)) / count
-    center = exact_dot(mean, group_spread(channels))[0:1]
-
-    def add_squares(i, spread):
-        away = (up_ref[i].astype(F32).reshape(-1, channels) - center).reshape(-1, 8, channels)
-        return spread + jnp.sum(away * away, axis=0)
-
-    spread = lax.fori_loop(0, share, add_squares, jnp.zeros((8, channels), F32))
-    spread = jnp.broadcast_to(jnp.sum(spread, axis=0, keepdims=True), (8, channels))
-    stats_ref[...] = (mean + exact_dot(spread, group_matrix(channels, LANES // 2)))[0:1]
-
-
-def upsample(block, conv_weight, share):
+        for parity, frames in enumerate((even, odd)):
+            piece = frames[j * length : (j + 1) * length]
+            up_ref[j, parity] = piece
+            away = piece.astype(F32) - center
+            shifts += jnp.sum(away.reshape(-1, fold, channels), axis=0)
+            squares += jnp.sum((away * away).reshape(-1, fold, channels), axis=0)
+    sums = jnp.concatenate([column_sums([shifts]), column_sums([squares])], axis=0)
+    sums = exact_dot(sums, group_matrix(channels, 0))
+    shift, square = sums[0:1], sums[8:9]
+    own = pivot[0:1] + shift / count + pltpu.roll(square - shift * shift / count, LANES // 2, 1)
+    stats_ref[...] = jnp.broadcast_to(own, stats_ref.shape)
+
+
+def upsample(block, conv_weight, share, copies):
     devices, rows, channels = block.shape
     length = devices * (rows // (share + 2))
     return pl.pallas_call(
         functools.partial(upsample_kernel, share),
         out_shape=(
             jax.ShapeDtypeStruct((share, 2, length, channels), BF16),
-            jax.ShapeDtypeStruct((1, LANES), F32),
+            jax.ShapeDtypeStruct((copies, LANES), F32),
         ),
         scratch_shapes=[pltpu.VMEM((3, share * length, channels), BF16)],
         compiler_params=params(48),
@@ -152,16 +154,15 @@
     return both[0:1], lax.rsqrt(both[8:9] + EPSILON) * gain.astype(F32)
 
 
-def attend_pixel(qkv):
-    rows, channels = qkv.shape[0], qkv.shape[1] // 3
+def attend_pixel(queries, keys, values):
+    rows, channels = queries.shape
     heads = channels // HEAD_DIM
     head = lax.broadcasted_iota(jnp.int32, (rows, channels), 1) // HEAD_DIM
     first = lax.broadcasted_iota(jnp.int32, (rows, LANES), 1) < HEAD_DIM
-    queries, keys, values = (qkv[:, i * channels : (i + 1) * channels] for i in range(3))
     zeros = jnp.zeros_like(queries)
     stacked = jnp.concatenate([jnp.where(head == h, queries, zeros) for h in range(heads)], axis=0)
     scores = lax.dot_general(stacked, keys, NT, preferred_element_type=F32)
-    ones = jnp.ones((rows, LANES), BF16)
+    ones = jnp.ones((keys.shape[0], LANES), BF16)
     context = []
     for pair in range(heads // 2):
         part = scores[pair * 2 * rows : (pair + 1) * 2 * rows]
@@ -177,14 +178,40 @@
     return jnp.concatenate(context, axis=1)
 
 
-def attend_kernel(
-    count, batch, up_ref, stats_ref, gain_ref, block_ref, qkv_ref, out_weight_ref, out_ref, embed, projected, context
+def attend_targets(steps, up_ref, projected, out_weight_ref, out_refs, context):
+    share, _, length, channels = up_ref.shape
+    part = out_refs[0].shape[2]
+    me = lax.axis_index("frames")
+    starts = [
+        pl.multiple_of(parity * length + (me ^ k) * part, part) for k in steps for parity in range(2)
+    ]
+    rows = len(starts) * part
+    for j in range(share):
+        base = j * 2 * length
+        queries = jnp.concatenate([projected[pl.ds(base + s, part), 0:channels] for s in starts], axis=0)
+        keys = projected[base : base + 2 * length, channels : 2 * channels]
+        values = projected[base : base + 2 * length, 2 * channels : 3 * channels]
+        context[j * rows : (j + 1) * rows, :] = attend_pixel(queries, keys, values)
+    mixed = jnp.dot(context[0 : share * rows, :], out_weight_ref[...], preferred_element_type=F32)
+    for j in range(share):
+        for i, k in enumerate(steps):
+            for parity in range(2):
+                place = 2 * i + parity
+                start = pl.multiple_of((me ^ k) * part, part)
+                up = up_ref[j, parity, pl.ds(start, part), :].astype(F32)
+                first = j * rows + place * part
+                out_refs[i][j, parity] = (up + mixed[first : first + part]).astype(BF16)
+
+
+def attend_first_kernel(
+    steps, count, batch, up_ref, stats_ref, gain_ref, block_ref, qkv_ref, out_weight_ref, *refs
 ):
+    *out_refs, projected, embed, context = refs
     share, _, length, channels = up_ref.shape
     devices = block_ref.shape[0]
     part = length // devices
     frames = 2 * length
-    center, scale = moments(stats_ref[...].reshape(-1, LANES), count, gain_ref[...])
+    center, scale = moments(stats_ref[...], count, gain_ref[...])
     base = share * part
     for parity in range(2):
         for s in range(devices):
@@ -206,63 +233,97 @@
     lax.fori_loop(0, share // batch, project_batch, 0)
     if share % batch:
         project(share - share % batch, share % batch)
-    for j in range(share):
-        rows = slice(j * frames, (j + 1) * frames)
-        context[rows, :] = attend_pixel(projected[rows, :])
-    mixed = jnp.dot(context[...], out_weight_ref[...], preferred_element_type=F32)
-    for j in range(share):
-        up = up_ref[j].reshape(frames, channels).astype(F32)
-        blended = (up + mixed[j * frames : (j + 1) * frames]).astype(BF16)
-        for d in range(devices):
-            for parity in range(2):
-                start = parity * length + d * part
-                out_ref[d, j, parity] = blended[start : start + part]
-
-
-def attend(up, stats, norm_gain, block, qkv_weight, out_weight):
+    attend_targets(steps, up_ref, projected, out_weight_ref, out_refs, context)
+
+
+def attend_rest_kernel(steps, up_ref, projected, out_weight_ref, *refs):
+    *out_refs, context = refs
+    attend_targets(steps, up_ref, projected, out_weight_ref, out_refs, context)
+
+
+def attend_cost(share, length, channels, steps, part):
+    rows = share * 2 * part * steps
+    flops = 2 * rows * channels * (2 * length * 8 + channels)
+    return pl.CostEstimate(flops=flops, bytes_accessed=rows * channels * 4, transcendentals=rows * 8 * length)
+
+
+def attend_first(steps, up, stats, norm_gain, block, qkv_weight, out_weight):
     share, _, length, channels = up.shape
     devices = block.shape[0]
     part = length // devices
     count = share * 2 * length * (channels // GROUPS)
     rows = share * 2 * length
-    return pl.pallas_call(
-        functools.partial(attend_kernel, count, 4),
-        out_shape=jax.ShapeDtypeStruct((devices, share, 2, part, channels), BF16),
+    piece = jax.ShapeDtypeStruct((share, 2, part, channels), BF16)
+    return pl.pallas_call(
+        functools.partial(attend_first_kernel, steps, count, 4),
+        out_shape=(piece,) * len(steps) + (jax.ShapeDtypeStruct((rows, 3 * channels), BF16),),
         scratch_shapes=[
             pltpu.VMEM((2 * length, channels), F32),
-            pltpu.VMEM((rows, 3 * channels), BF16),
-            pltpu.VMEM((rows, channels), BF16),
+            pltpu.VMEM((share * 2 * part * len(steps), channels), BF16),
         ],
-        compiler_params=params(48),
-        name="attend",
+        compiler_params=params(40),
+        cost_estimate=attend_cost(share, length, channels, len(steps), part),
+        name="attend_first",
     )(up, stats, norm_gain.reshape(1, channels), block, qkv_weight, out_weight)
 
 
-def unpack_kernel(block_ref, out_ref, wide):
-    devices, share, _, part, _ = block_ref.shape
-    frames, pixels, _ = out_ref.shape
+def attend_rest(steps, up, projected, out_weight, part):
+    share, _, length, channels = up.shape
+    piece = jax.ShapeDtypeStruct((share, 2, part, channels), BF16)
+    return pl.pallas_call(
+        functools.partial(attend_rest_kernel, steps),
+        out_shape=(piece,) * len(steps),
+        scratch_shapes=[pltpu.VMEM((share * 2 * part * len(steps), channels), BF16)],
+        compiler_params=params(40),
+        cost_estimate=attend_cost(share, length, channels, len(steps), part),
+        name="attend_rest",
+    )(up, projected, out_weight)
+
+
+def unpack_kernel(steps, *refs):
+    *block_refs, out_hbm, held, wide, sems = refs
+    frames, pixels, _ = held.shape
+    pieces = sems.shape[1]
+    step = frames // pieces
+    copies = []
+    share, _, part, _ = block_refs[0].shape
+    me = lax.axis_index("frames")
     for half in range(wide.shape[0]):
         lanes = slice(half * LANES, (half + 1) * LANES)
-        for s in range(devices):
+        for k, block_ref in zip(steps, block_refs):
             for j in range(share):
                 for parity in range(2):
-                    start = parity * pixels + s * share + j
-                    rows = block_ref[s, j, parity, :, lanes].astype(F32)
+                    start = parity * pixels + j + (me ^ k) * share
+                    rows = block_ref[j, parity, :, lanes].astype(F32)
                     wide[half, pl.ds(start, part, stride=2 * pixels), :] = rows
-        for f in range(frames):
-            out_ref[f, :, lanes] = wide[half, f * pixels : (f + 1) * pixels, :].astype(BF16)
-
-
-def unpack(block):
-    devices, share, _, part, channels = block.shape
-    frames, pixels = 2 * part, devices * share
-    return pl.pallas_call(
-        unpack_kernel,
+        for i in range(pieces):
+            for f in range(i * step, (i + 1) * step):
+                held[f, :, lanes] = wide[half, f * pixels : (f + 1) * pixels, :].astype(BF16)
+            span = (pl.ds(i * step, step), slice(None), pl.ds(half * LANES, LANES))
+            copies.append(pltpu.make_async_copy(held.at[span], out_hbm.at[span], sems.at[half, i]))
+            copies[-1].start()
+    for copy in copies:
+        copy.wait()
+
+
+def unpack(steps, blocks):
+    share, _, part, channels = blocks[0].shape
+    frames, pixels = 2 * part, len(blocks) * share
+    return pl.pallas_call(
+        functools.partial(unpack_kernel, steps),
         out_shape=jax.ShapeDtypeStruct((frames, pixels, channels), BF16),
-        scratch_shapes=[pltpu.VMEM((channels // LANES, frames * pixels, LANES), F32)],
+        out_specs=pl.BlockSpec(memory_space=pltpu.HBM),
+        scratch_shapes=[
+            pltpu.VMEM((frames, pixels, channels), BF16),
+            pltpu.VMEM((channels // LANES, frames * pixels, LANES), F32),
+            pltpu.SemaphoreType.DMA((channels // LANES, 4)),
+        ],
         compiler_params=params(24),
         name="unpack_output",
-    )(block)
+    )(*blocks)
+
+
+TARGETS = ((4, 2), (6, 7, 5), (1, 3, 0))
 
 
 def per_device(latent, conv_weight, norm_gain, frame_embed, qkv_weight, out_weight):
@@ -271,12 +332,18 @@
     share = latent.shape[1] // devices
     sent = pack(latent, frame_embed, devices)
     block = lax.all_to_all(sent, "frames", 0, 0)
-    up, stats = upsample(block, conv_weight, share)
-    stats = lax.all_to_all(
-        jnp.broadcast_to(stats[None], (everyone,) + stats.shape), ("rows", "frames"), 0, 0
-    )
-    blended = attend(up, stats, norm_gain, block, qkv_weight, out_weight)
-    return unpack(lax.all_to_all(blended, "frames", 0, 0))
+    up, copies = upsample(block, conv_weight, share, everyone)
+    stats = lax.all_to_all(copies, ("rows", "frames"), 0, 0)
+
+    def send(piece, k):
+        return lax.ppermute(piece, "frames", [(i, i ^ k) for i in range(devices)]) if k else piece
+
+    *pieces, projected = attend_first(TARGETS[0], up, stats, norm_gain, block, qkv_weight, out_weight)
+    got = [send(piece, k) for piece, k in zip(pieces, TARGETS[0])]
+    for steps in TARGETS[1:]:
+        pieces = attend_rest(steps, up, projected, out_weight, pieces[0].shape[2])
+        got += [send(piece, k) for piece, k in zip(pieces, steps)]
+    return unpack(sum(TARGETS, ()), got)
 
 
 def solution(mesh):

time: 78.8 us -> 72.8 us (0.924)
  blocking collectives: 47 us -> 21.4 us
  starting transfers between devices: 7.66 us -> 18 us
  waiting for transfers between devices: 9.21 us -> 17.4 us
  Pallas kernels: 12 us -> 13.8 us
    all_to_all x1 -> x0, blocking collectives: 25.6 us -> none  [per_device(): return unpack(lax.all_to_all(blended, 'frames', 0, 0))]
    ppermute x0 -> x7, starting transfers between devices: none -> 10.3 us  [send(): lax.ppermute(piece, 'frames', [(i, i ^ k) for i in range(devices)])]
    ppermute x0 -> x7, waiting for transfers between devices: none -> 8.16 us  [send(): lax.ppermute(piece, 'frames', [(i, i ^ k) for i in range(devices)])]
    pallas_call x2 -> x4, Pallas kernels: 8.88 us -> 10.3 us  [the longest x2 4.24 us: attend_rest(): pl.pallas_call(functools.partial(attend_rest_kernel, steps), out_shape=(p...]
  transfers between devices with their start and end apart: 1 -> 8, of which waited for: 1 -> 5; matrix products, arithmetic and copies ran while one was open for 0% -> 0% of each run, Pallas kernels for 0% -> 6%
where the time goes in v3:
time: 72.8 us; the launch traced here: 72.6 us
  blocking collectives  21.4 us (29%)
  starting transfers between devices  18 us (25%)
  waiting for transfers between devices  17.4 us (24%)
  Pallas kernels  13.8 us (19%)
  local copies, waits for them, and re-layouts  1.9 us (3%)
    all_to_all x1, blocking collectives, per_device(): block = lax.all_to_all(sent, 'frames', 0, 0)  21.4 us
    ppermute x7, starting transfers between devices, send(): lax.ppermute(piece, 'frames', [(i, i ^ k) for i in range(devices)])  10.3 us
    all_to_all x1, waiting for transfers between devices, per_device(): stats = lax.all_to_all(copies, ('rows', 'frames'), 0, 0)  9.21 us
    ppermute x7, waiting for transfers between devices, send(): lax.ppermute(piece, 'frames', [(i, i ^ k) for i in range(devices)])  8.16 us
    all_to_all x1, starting transfers between devices, per_device(): stats = lax.all_to_all(copies, ('rows', 'frames'), 0, 0)  7.67 us
    pallas_call x2, Pallas kernels, attend_rest(): pl.pallas_call(functools.partial(attend_rest_kernel, steps), out_shape=(p...  4.24 us
    pallas_call x1, Pallas kernels, attend_first(): pl.pallas_call(functools.partial(attend_first_kernel, steps, count, 4), o...  3.87 us
    pallas_call x1, Pallas kernels, upsample(): pl.pallas_call(functools.partial(upsample_kernel, share), out_shape=(jax....  2.98 us
  transfers between devices with their start and end apart: 8, of which 5 were waited for; matrix products, arithmetic and copies ran while one was open for 0% of the time, Pallas kernels for 6%

profile of v3, /device:TPU:0, one launch (start us, length us, event | category | flops | bytes accessed | tf_op | source)
XLA Modules:
  0.0 72.6 jit_solution(9349986345224246457)
XLA Ops:
  0.0 1.2 %copy-done = bf16[16,104,256]{2,1,0:T(8,128)(2,1)S(1)} copy-done((bf16[16,104,256]{2,1,0:T(8,128)(2,1)S(1)}, bf16[16,104,256]{2,1,0:T(8,128)(2,1)}, u32[]{:S(2)}) %copy-start) | copy-done | bytes 851992
  1.2 0.7 copy-done.3
  1.9 0.4 pack_latent.1
  2.3 0.0 copy-start.5
  2.3 0.0 copy-start.4
  2.4 21.4 %all_to_all.16.block_ref = bf16[8,240,256]{2,1,0:T(8,128)(2,1)S(1)} all-to-all(bf16[8,240,256]{2,1,0:T(8,128)(2,1)S(1)} %pack_latent.1), channel_id=1, replica_groups=mesh['rows'=16,'frames'=8] {'frames'}, dimensions={0} | all-to-all | bytes 1966080 | tf_op jit(solution)/shard_map/all_to_all | solution.py:334
  23.8 3.0 %upsample.1 = (bf16[13,2,128,256]{3,2,1,0:T(8,128)(2,1)S(1)}, f32[128,128]{1,0:T(8,128)}) custom-call(bf16[8,240,256]{2,1,0:T(8,128)(2,1)S(1)} %all_to_all.16.block_ref, bf16[4,256,256]{2,1,0:T(8,128)(2,1)S(1)} %copy-done.1), custom_call_target="tpu_custom_call" | custom-call | tf_op jit(solution)/shard_map/upsample/pallas_call | solution.py:128
  26.8 7.7 %all-to-all-start.1 = ((f32[128,1,128]{2,1,0:T(1,128)}), f32[128,1,128]{2,1,0:T(1,128)S(1)}, u32[]{:S(2)}, u32[]{:S(2)}) async-start(f32[128,1,128]{2,1,0:T(1,128)} %bitcast.1), calls=%async_computation.1 | async-start | bytes 131072 | tf_op jit(solution)/shard_map/all_to_all | solution.py:336
  34.5 9.2 %all-to-all-done.1 = f32[128,1,128]{2,1,0:T(1,128)S(1)} async-done(((f32[128,1,128]{2,1,0:T(1,128)}), f32[128,1,128]{2,1,0:T(1,128)S(1)}, u32[]{:S(2)}, u32[]{:S(2)}) %all-to-all-start.1) | async-done | bytes 65568 | tf_op jit(solution)/shard_map/all_to_all | solution.py:336
  43.7 3.9 %attend_first.1 = (bf16[13,2,16,256]{3,2,1,0:T(8,128)(2,1)S(1)}, bf16[13,2,16,256]{3,2,1,0:T(8,128)(2,1)S(1)}, bf16[3328,768]{1,0:T(8,128)(2,1)S(1)}) custom-call(bf16[13,2,128,256]{3,2,1,0:T(8,128)(2,1)S(1)} %get-tuple-element.16.up_ref, f32[128,128]{1,0:T(8,128)S(1)} %bitcast.4, bf16[1,256]{1,0:T(2,128)(2,1)S(1)} %reshape.5.gain_ref, ...), custom_call_target="tpu_custom_call" | custom-call | flops 981467136 | bytes 851968 | tf_op jit(solution)/shard_map/attend_first/pallas_call | solution.py:257
  47.6 0.5 collective-permute-start
  48.0 1.5 %collective-permute-start.1 = (bf16[13,2,16,256]{3,2,1,0:T(8,128)(2,1)S(1)}, bf16[13,2,16,256]{3,2,1,0:T(8,128)(2,1)S(1)}, u32[]{:S(2)}, u32[]{:S(2)}) collective-permute-start(bf16[13,2,16,256]{3,2,1,0:T(8,128)(2,1)S(1)} %get-tuple-element.19), channel_id=1, source_target_pairs={{0,2},{1,3},{2,0},{3,1},{4,6},{5,7},{6,4},{7,5},{8,10},{9,11},{10,... | collective-permute-start | bytes 638984 | tf_op jit(solution)/shard_map/ppermute | solution.py:339
  49.5 2.1 %attend_rest.2 = (bf16[13,2,16,256]{3,2,1,0:T(8,128)(2,1)S(1)}, bf16[13,2,16,256]{3,2,1,0:T(8,128)(2,1)S(1)}, bf16[13,2,16,256]{3,2,1,0:T(8,128)(2,1)S(1)}) custom-call(bf16[13,2,128,256]{3,2,1,0:T(8,128)(2,1)S(1)} %get-tuple-element.16.up_ref, bf16[3328,768]{1,0:T(8,128)(2,1)S(1)} %get-tuple-element.20.projected, bf16[256,256]{1,0:T(8,128)(2,1)S(1)} %copy-done.2), custom_call_target="tpu_custom_call" | custom-call | flops 1472200704 | bytes 1277952 | tf_op jit(solution)/shard_map/attend_rest/pallas_call | solution.py:273
  51.7 3.2 %collective-permute-start.2 = (bf16[13,2,16,256]{3,2,1,0:T(8,128)(2,1)S(1)}, bf16[13,2,16,256]{3,2,1,0:T(8,128)(2,1)S(1)}, u32[]{:S(2)}, u32[]{:S(2)}) collective-permute-start(bf16[13,2,16,256]{3,2,1,0:T(8,128)(2,1)S(1)} %get-tuple-element.21), channel_id=1, source_target_pairs={{0,6},{1,7},{2,4},{3,5},{4,2},{5,3},{6,0},{7,1},{8,14},{9,15},{10,... | collective-permute-start | bytes 638984 | tf_op jit(solution)/shard_map/ppermute | solution.py:339
  54.8 0.8 %collective-permute-start.3 = (bf16[13,2,16,256]{3,2,1,0:T(8,128)(2,1)S(1)}, bf16[13,2,16,256]{3,2,1,0:T(8,128)(2,1)S(1)}, u32[]{:S(2)}, u32[]{:S(2)}) collective-permute-start(bf16[13,2,16,256]{3,2,1,0:T(8,128)(2,1)S(1)} %get-tuple-element.22), channel_id=1, source_target_pairs={{0,7},{1,6},{2,5},{3,4},{4,3},{5,2},{6,1},{7,0},{8,15},{9,14},{10,... | collective-permute-start | bytes 638984 | tf_op jit(solution)/shard_map/ppermute | solution.py:339
  55.7 1.3 %collective-permute-start.4 = (bf16[13,2,16,256]{3,2,1,0:T(8,128)(2,1)S(1)}, bf16[13,2,16,256]{3,2,1,0:T(8,128)(2,1)S(1)}, u32[]{:S(2)}, u32[]{:S(2)}) collective-permute-start(bf16[13,2,16,256]{3,2,1,0:T(8,128)(2,1)S(1)} %get-tuple-element.23), channel_id=1, source_target_pairs={{0,5},{1,4},{2,7},{3,6},{4,1},{5,0},{6,3},{7,2},{8,13},{9,12},{10,... | collective-permute-start | bytes 638984 | tf_op jit(solution)/shard_map/ppermute | solution.py:339
  57.0 2.1 %attend_rest.3 = (bf16[13,2,16,256]{3,2,1,0:T(8,128)(2,1)S(1)}, bf16[13,2,16,256]{3,2,1,0:T(8,128)(2,1)S(1)}, bf16[13,2,16,256]{3,2,1,0:T(8,128)(2,1)S(1)}) custom-call(bf16[13,2,128,256]{3,2,1,0:T(8,128)(2,1)S(1)} %get-tuple-element.16.up_ref, bf16[3328,768]{1,0:T(8,128)(2,1)S(1)} %get-tuple-element.20.projected, bf16[256,256]{1,0:T(8,128)(2,1)S(1)} %copy-done.2), custom_call_target="tpu_custom_call" | custom-call | flops 1472200704 | bytes 1277952 | tf_op jit(solution)/shard_map/attend_rest/pallas_call | solution.py:273
  59.1 1.6 %collective-permute-start.5 = (bf16[13,2,16,256]{3,2,1,0:T(8,128)(2,1)S(1)}, bf16[13,2,16,256]{3,2,1,0:T(8,128)(2,1)S(1)}, u32[]{:S(2)}, u32[]{:S(2)}) collective-permute-start(bf16[13,2,16,256]{3,2,1,0:T(8,128)(2,1)S(1)} %get-tuple-element.24), channel_id=1, source_target_pairs={{0,1},{1,0},{2,3},{3,2},{4,5},{5,4},{6,7},{7,6},{8,9},{9,8},{10,11... | collective-permute-start | bytes 638984 | tf_op jit(solution)/shard_map/ppermute | solution.py:339
  60.8 1.0 %collective-permute-done.1.refs_1_ = bf16[13,2,16,256]{3,2,1,0:T(8,128)(2,1)S(1)} collective-permute-done((bf16[13,2,16,256]{3,2,1,0:T(8,128)(2,1)S(1)}, bf16[13,2,16,256]{3,2,1,0:T(8,128)(2,1)S(1)}, u32[]{:S(2)}, u32[]{:S(2)}) %collective-permute-start.1) | collective-permute-done | bytes 213024 | tf_op jit(solution)/shard_map/ppermute | solution.py:339
  61.8 1.4 %collective-permute-start.6 = (bf16[13,2,16,256]{3,2,1,0:T(8,128)(2,1)S(1)}, bf16[13,2,16,256]{3,2,1,0:T(8,128)(2,1)S(1)}, u32[]{:S(2)}, u32[]{:S(2)}) collective-permute-start(bf16[13,2,16,256]{3,2,1,0:T(8,128)(2,1)S(1)} %get-tuple-element.25), channel_id=1, source_target_pairs={{0,3},{1,2},{2,1},{3,0},{4,7},{5,6},{6,5},{7,4},{8,11},{9,10},{10,... | collective-permute-start | bytes 638984 | tf_op jit(solution)/shard_map/ppermute | solution.py:339
  63.2 3.8 %collective-permute-done.3.refs_3_ = bf16[13,2,16,256]{3,2,1,0:T(8,128)(2,1)S(1)} collective-permute-done((bf16[13,2,16,256]{3,2,1,0:T(8,128)(2,1)S(1)}, bf16[13,2,16,256]{3,2,1,0:T(8,128)(2,1)S(1)}, u32[]{:S(2)}, u32[]{:S(2)}) %collective-permute-start.3) | collective-permute-done | bytes 213024 | tf_op jit(solution)/shard_map/ppermute | solution.py:339
  67.0 3.0 %collective-permute-done.4.refs_4_ = bf16[13,2,16,256]{3,2,1,0:T(8,128)(2,1)S(1)} collective-permute-done((bf16[13,2,16,256]{3,2,1,0:T(8,128)(2,1)S(1)}, bf16[13,2,16,256]{3,2,1,0:T(8,128)(2,1)S(1)}, u32[]{:S(2)}, u32[]{:S(2)}) %collective-permute-start.4) | collective-permute-done | bytes 213024 | tf_op jit(solution)/shard_map/ppermute | solution.py:339
  70.0 0.3 collective-permute-done.6.refs_6_
  70.3 2.2 %unpack_output.1 = bf16[32,104,256]{2,1,0:T(8,128)(2,1)} custom-call(bf16[13,2,16,256]{3,2,1,0:T(8,128)(2,1)S(1)} %collective-permute-done.refs_0_, bf16[13,2,16,256]{3,2,1,0:T(8,128)(2,1)S(1)} %collective-permute-done.1.refs_1_, bf16[13,2,16,256]{3,2,1,0:T(8,128)(2,1)S(1)} %collective-permute-done.2.refs_2_, ...), custom_call_target="tpu_custom_call" | custom-call | tf_op jit(solution)/shard_map/unpack_output/pallas_call | solution.py:312
  (12 shorter events, 0.0 us)
Async XLA Ops:
  0.0 1.2 %copy-start = (bf16[16,104,256]{2,1,0:T(8,128)(2,1)S(1)}, bf16[16,104,256]{2,1,0:T(8,128)(2,1)}, u32[]{:S(2)}) copy-start(bf16[16,104,256]{2,1,0:T(8,128)(2,1)} %latent_ref.1) | copy-start | bytes 2555908
  1.2 0.7 copy-start.3
  1.9 21.9 %copy-start.1 = (bf16[4,256,256]{2,1,0:T(8,128)(2,1)S(1)}, bf16[4,256,256]{2,1,0:T(8,128)(2,1)}, u32[]{:S(2)}) copy-start(bf16[4,256,256]{2,1,0:T(8,128)(2,1)} %conv_ref.1) | copy-start | bytes 1572868
  2.3 32.1 %copy-start.5 = (bf16[256]{0:T(256)(128)(2,1)S(1)}, bf16[256]{0:T(256)(128)(2,1)}, u32[]{:S(2)}) copy-start(bf16[256]{0:T(256)(128)(2,1)} %param.8) | copy-start | bytes 1540
  2.3 41.4 %copy-start.2 = (bf16[256,256]{1,0:T(8,128)(2,1)S(1)}, bf16[256,256]{1,0:T(8,128)(2,1)}, u32[]{:S(2)}) copy-start(bf16[256,256]{1,0:T(8,128)(2,1)} %out_weight_ref.5) | copy-start | bytes 393220
  2.3 41.3 %copy-start.4 = (bf16[256,768]{1,0:T(8,128)(2,1)S(1)}, bf16[256,768]{1,0:T(8,128)(2,1)}, u32[]{:S(2)}) copy-start(bf16[256,768]{1,0:T(8,128)(2,1)} %qkv_ref.1) | copy-start | bytes 1179652
  26.8 16.9 %all-to-all-start.1 = ((f32[128,1,128]{2,1,0:T(1,128)}), f32[128,1,128]{2,1,0:T(1,128)S(1)}, u32[]{:S(2)}, u32[]{:S(2)}) async-start(f32[128,1,128]{2,1,0:T(1,128)} %bitcast.1), calls=%async_computation.1 | async-start | bytes 131072 | tf_op jit(solution)/shard_map/all_to_all | solution.py:336
  47.6 11.5 %collective-permute-start = (bf16[13,2,16,256]{3,2,1,0:T(8,128)(2,1)S(1)}, bf16[13,2,16,256]{3,2,1,0:T(8,128)(2,1)S(1)}, u32[]{:S(2)}, u32[]{:S(2)}) collective-permute-start(bf16[13,2,16,256]{3,2,1,0:T(8,128)(2,1)S(1)} %get-tuple-element.18), channel_id=1, source_target_pairs={{0,4},{1,5},{2,6},{3,7},{4,0},{5,1},{6,2},{7,3},{8,12},{9,13},{10,... | collective-permute-start | bytes 638984 | tf_op jit(solution)/shard_map/ppermute | solution.py:339
  48.0 13.8 %collective-permute-start.1 = (bf16[13,2,16,256]{3,2,1,0:T(8,128)(2,1)S(1)}, bf16[13,2,16,256]{3,2,1,0:T(8,128)(2,1)S(1)}, u32[]{:S(2)}, u32[]{:S(2)}) collective-permute-start(bf16[13,2,16,256]{3,2,1,0:T(8,128)(2,1)S(1)} %get-tuple-element.19), channel_id=1, source_target_pairs={{0,2},{1,3},{2,0},{3,1},{4,6},{5,7},{6,4},{7,5},{8,10},{9,11},{10,... | collective-permute-start | bytes 638984 | tf_op jit(solution)/shard_map/ppermute | solution.py:339
  51.7 11.6 %collective-permute-start.2 = (bf16[13,2,16,256]{3,2,1,0:T(8,128)(2,1)S(1)}, bf16[13,2,16,256]{3,2,1,0:T(8,128)(2,1)S(1)}, u32[]{:S(2)}, u32[]{:S(2)}) collective-permute-start(bf16[13,2,16,256]{3,2,1,0:T(8,128)(2,1)S(1)} %get-tuple-element.21), channel_id=1, source_target_pairs={{0,6},{1,7},{2,4},{3,5},{4,2},{5,3},{6,0},{7,1},{8,14},{9,15},{10,... | collective-permute-start | bytes 638984 | tf_op jit(solution)/shard_map/ppermute | solution.py:339
  54.8 12.2 %collective-permute-start.3 = (bf16[13,2,16,256]{3,2,1,0:T(8,128)(2,1)S(1)}, bf16[13,2,16,256]{3,2,1,0:T(8,128)(2,1)S(1)}, u32[]{:S(2)}, u32[]{:S(2)}) collective-permute-start(bf16[13,2,16,256]{3,2,1,0:T(8,128)(2,1)S(1)} %get-tuple-element.22), channel_id=1, source_target_pairs={{0,7},{1,6},{2,5},{3,4},{4,3},{5,2},{6,1},{7,0},{8,15},{9,14},{10,... | collective-permute-start | bytes 638984 | tf_op jit(solution)/shard_map/ppermute | solution.py:339
  55.7 14.3 %collective-permute-start.4 = (bf16[13,2,16,256]{3,2,1,0:T(8,128)(2,1)S(1)}, bf16[13,2,16,256]{3,2,1,0:T(8,128)(2,1)S(1)}, u32[]{:S(2)}, u32[]{:S(2)}) collective-permute-start(bf16[13,2,16,256]{3,2,1,0:T(8,128)(2,1)S(1)} %get-tuple-element.23), channel_id=1, source_target_pairs={{0,5},{1,4},{2,7},{3,6},{4,1},{5,0},{6,3},{7,2},{8,13},{9,12},{10,... | collective-permute-start | bytes 638984 | tf_op jit(solution)/shard_map/ppermute | solution.py:339
  59.1 10.9 %collective-permute-start.5 = (bf16[13,2,16,256]{3,2,1,0:T(8,128)(2,1)S(1)}, bf16[13,2,16,256]{3,2,1,0:T(8,128)(2,1)S(1)}, u32[]{:S(2)}, u32[]{:S(2)}) collective-permute-start(bf16[13,2,16,256]{3,2,1,0:T(8,128)(2,1)S(1)} %get-tuple-element.24), channel_id=1, source_target_pairs={{0,1},{1,0},{2,3},{3,2},{4,5},{5,4},{6,7},{7,6},{8,9},{9,8},{10,11... | collective-permute-start | bytes 638984 | tf_op jit(solution)/shard_map/ppermute | solution.py:339
  61.8 8.5 %collective-permute-start.6 = (bf16[13,2,16,256]{3,2,1,0:T(8,128)(2,1)S(1)}, bf16[13,2,16,256]{3,2,1,0:T(8,128)(2,1)S(1)}, u32[]{:S(2)}, u32[]{:S(2)}) collective-permute-start(bf16[13,2,16,256]{3,2,1,0:T(8,128)(2,1)S(1)} %get-tuple-element.25), channel_id=1, source_target_pairs={{0,3},{1,2},{2,1},{3,0},{4,7},{5,6},{6,5},{7,4},{8,11},{9,10},{10,... | collective-permute-start | bytes 638984 | tf_op jit(solution)/shard_map/ppermute | solution.py:339

commit v4 on v3

--- a/solution.py
+++ b/solution.py
@@ -91,30 +91,36 @@
         taps[1, rows, :] = here
         taps[2, rows, :] = after.astype(BF16)
 
-    def tap(source, index):
-        return jnp.dot(taps[source], conv_ref[index], preferred_element_type=F32)
-
-    even = (tap(1, 1) + tap(0, 3)).astype(BF16)
-    odd = (tap(2, 0) + tap(1, 2)).astype(BF16)
     count = share * 2 * length * (channels // GROUPS)
-    fold = 32
+    fold = 16
 
     def column_sums(pieces):
         total = sum(jnp.sum(piece.reshape(-1, fold, channels), axis=0) for piece in pieces)
         return jnp.broadcast_to(jnp.sum(total, axis=0, keepdims=True), (8, channels))
 
-    pivot = column_sums([frames[0:length].astype(F32) for frames in (even, odd)])
-    pivot = exact_dot(pivot, group_matrix(channels, 0)) * (share / count)
-    center = exact_dot(pivot, group_spread(channels))[0:1]
     shifts = jnp.zeros((fold, channels), F32)
     squares = jnp.zeros((fold, channels), F32)
-    for j in range(share):
-        for parity, frames in enumerate((even, odd)):
-            piece = frames[j * length : (j + 1) * length]
-            up_ref[j, parity] = piece
-            away = piece.astype(F32) - center
-            shifts += jnp.sum(away.reshape(-1, fold, channels), axis=0)
-            squares += jnp.sum((away * away).reshape(-1, fold, channels), axis=0)
+    first = 0
+    for pixels in (1, 6, 6):
+        rows = slice(first * length, (first + pixels) * length)
+
+        def tap(source, index):
+            return jnp.dot(taps[source, rows, :], conv_ref[index], preferred_element_type=F32)
+
+        even = (tap(1, 1) + tap(0, 3)).astype(BF16)
+        odd = (tap(2, 0) + tap(1, 2)).astype(BF16)
+        if first == 0:
+            pivot = column_sums([frames[0:length].astype(F32) for frames in (even, odd)])
+            pivot = exact_dot(pivot, group_matrix(channels, 0)) * (share / count)
+            center = exact_dot(pivot, group_spread(channels))[0:1]
+        for j in range(pixels):
+            for parity, frames in enumerate((even, odd)):
+                piece = frames[j * length : (j + 1) * length]
+                up_ref[first + j, parity] = piece
+                away = piece.astype(F32) - center
+                shifts += jnp.sum(away.reshape(-1, fold, channels), axis=0)
+                squares += jnp.sum((away * away).reshape(-1, fold, channels), axis=0)
+        first += pixels
     sums = jnp.concatenate([column_sums([shifts]), column_sums([squares])], axis=0)
     sums = exact_dot(sums, group_matrix(channels, 0))
     shift, square = sums[0:1], sums[8:9]
@@ -162,23 +168,20 @@
     zeros = jnp.zeros_like(queries)
     stacked = jnp.concatenate([jnp.where(head == h, queries, zeros) for h in range(heads)], axis=0)
     scores = lax.dot_general(stacked, keys, NT, preferred_element_type=F32)
-    ones = jnp.ones((keys.shape[0], LANES), BF16)
+    top = jnp.max(scores, axis=1, keepdims=True)
+    weights = jnp.exp2((scores - top) * (LOG2E * HEAD_DIM**-0.5))
+    scale = 1.0 / jnp.sum(weights, axis=1, keepdims=True)
+    mixed = jnp.dot(weights.astype(BF16), values, preferred_element_type=F32)
     context = []
     for pair in range(heads // 2):
-        part = scores[pair * 2 * rows : (pair + 1) * 2 * rows]
-        top = jnp.max(part, axis=1, keepdims=True)
-        weights = jnp.exp2((part - top) * (LOG2E * HEAD_DIM**-0.5)).astype(BF16)
-        value = jnp.concatenate([values[:, pair * LANES : (pair + 1) * LANES], ones], axis=1)
-        sums = jnp.dot(weights, value, preferred_element_type=F32)
-        above, total = (
-            jnp.where(first, sums[:rows, i * LANES : (i + 1) * LANES], sums[rows:, i * LANES : (i + 1) * LANES])
-            for i in range(2)
-        )
-        context.append((above * (1.0 / total)).astype(BF16))
+        lanes = slice(pair * LANES, (pair + 1) * LANES)
+        upper, lower = (slice((2 * pair + i) * rows, (2 * pair + i + 1) * rows) for i in range(2))
+        part = jnp.where(first, mixed[upper, lanes], mixed[lower, lanes])
+        context.append((part * jnp.where(first, scale[upper], scale[lower])).astype(BF16))
     return jnp.concatenate(context, axis=1)
 
 
-def attend_targets(steps, up_ref, projected, out_weight_ref, out_refs, context):
+def attend_targets(steps, up_ref, normed, keyed, qkv_ref, out_weight_ref, out_refs, queries, context):
     share, _, length, channels = up_ref.shape
     part = out_refs[0].shape[2]
     me = lax.axis_index("frames")
@@ -187,12 +190,17 @@
     ]
     rows = len(starts) * part
     for j in range(share):
-        base = j * 2 * length
-        queries = jnp.concatenate([projected[pl.ds(base + s, part), 0:channels] for s in starts], axis=0)
-        keys = projected[base : base + 2 * length, channels : 2 * channels]
-        values = projected[base : base + 2 * length, 2 * channels : 3 * channels]
-        context[j * rows : (j + 1) * rows, :] = attend_pixel(queries, keys, values)
-    mixed = jnp.dot(context[0 : share * rows, :], out_weight_ref[...], preferred_element_type=F32)
+        for i, start in enumerate(starts):
+            first = j * rows + i * part
+            queries[first : first + part, :] = normed[pl.ds(j * 2 * length + start, part), :]
+    queries[...] = jnp.dot(queries[...], qkv_ref[:, 0:channels], preferred_element_type=F32).astype(BF16)
+    for j in range(share):
+        span = slice(j * rows, (j + 1) * rows)
+        whole = slice(j * 2 * length, (j + 1) * 2 * length)
+        context[span, :] = attend_pixel(
+            queries[span, :], keyed[whole, 0:channels], keyed[whole, channels : 2 * channels]
+        )
+    mixed = jnp.dot(context[...], out_weight_ref[...], preferred_element_type=F32)
     for j in range(share):
         for i, k in enumerate(steps):
             for parity in range(2):
@@ -206,7 +214,7 @@
 def attend_first_kernel(
     steps, count, batch, up_ref, stats_ref, gain_ref, block_ref, qkv_ref, out_weight_ref, *refs
 ):
-    *out_refs, projected, embed, context = refs
+    *out_refs, normed_ref, keyed, embed, queries, context = refs
     share, _, length, channels = up_ref.shape
     devices = block_ref.shape[0]
     part = length // devices
@@ -224,7 +232,8 @@
         up = up_ref[pl.ds(first, pixels)].reshape(pixels, frames, channels).astype(F32)
         normed = ((up - center) * scale + embed[...]).astype(BF16).reshape(pixels * frames, channels)
         rows = pl.ds(pl.multiple_of(first * frames, frames), pixels * frames)
-        projected[rows, :] = jnp.dot(normed, qkv_ref[...], preferred_element_type=F32).astype(BF16)
+        normed_ref[rows, :] = normed
+        keyed[rows, :] = jnp.dot(normed, qkv_ref[:, channels:], preferred_element_type=F32).astype(BF16)
 
     def project_batch(i, carry):
         project(i * batch, batch)
@@ -233,12 +242,12 @@
     lax.fori_loop(0, share // batch, project_batch, 0)
     if share % batch:
         project(share - share % batch, share % batch)
-    attend_targets(steps, up_ref, projected, out_weight_ref, out_refs, context)
-
-
-def attend_rest_kernel(steps, up_ref, projected, out_weight_ref, *refs):
-    *out_refs, context = refs
-    attend_targets(steps, up_ref, projected, out_weight_ref, out_refs, context)
+    attend_targets(steps, up_ref, normed_ref, keyed, qkv_ref, out_weight_ref, out_refs, queries, context)
+
+
+def attend_rest_kernel(steps, up_ref, normed_ref, keyed, qkv_ref, out_weight_ref, *refs):
+    *out_refs, queries, context = refs
+    attend_targets(steps, up_ref, normed_ref, keyed, qkv_ref, out_weight_ref, out_refs, queries, context)
 
 
 def attend_cost(share, length, channels, steps, part):
@@ -256,9 +265,11 @@
     piece = jax.ShapeDtypeStruct((share, 2, part, channels), BF16)
     return pl.pallas_call(
         functools.partial(attend_first_kernel, steps, count, 4),
-        out_shape=(piece,) * len(steps) + (jax.ShapeDtypeStruct((rows, 3 * channels), BF16),),
+        out_shape=(piece,) * len(steps)
+        + (jax.ShapeDtypeStruct((rows, channels), BF16), jax.ShapeDtypeStruct((rows, 2 * channels), BF16)),
         scratch_shapes=[
             pltpu.VMEM((2 * length, channels), F32),
+            pltpu.VMEM((share * 2 * part * len(steps), channels), BF16),
             pltpu.VMEM((share * 2 * part * len(steps), channels), BF16),
         ],
         compiler_params=params(40),
@@ -267,17 +278,17 @@
     )(up, stats, norm_gain.reshape(1, channels), block, qkv_weight, out_weight)
 
 
-def attend_rest(steps, up, projected, out_weight, part):
+def attend_rest(steps, up, normed, keyed, qkv_weight, out_weight, part):
     share, _, length, channels = up.shape
     piece = jax.ShapeDtypeStruct((share, 2, part, channels), BF16)
     return pl.pallas_call(
         functools.partial(attend_rest_kernel, steps),
         out_shape=(piece,) * len(steps),
-        scratch_shapes=[pltpu.VMEM((share * 2 * part * len(steps), channels), BF16)],
+        scratch_shapes=[pltpu.VMEM((share * 2 * part * len(steps), channels), BF16)] * 2,
         compiler_params=params(40),
         cost_estimate=attend_cost(share, length, channels, len(steps), part),
         name="attend_rest",
-    )(up, projected, out_weight)
+    )(up, normed, keyed, qkv_weight, out_weight)
 
 
 def unpack_kernel(steps, *refs):
@@ -338,10 +349,10 @@
     def send(piece, k):
         return lax.ppermute(piece, "frames", [(i, i ^ k) for i in range(devices)]) if k else piece
 
-    *pieces, projected = attend_first(TARGETS[0], up, stats, norm_gain, block, qkv_weight, out_weight)
+    *pieces, normed, keyed = attend_first(TARGETS[0], up, stats, norm_gain, block, qkv_weight, out_weight)
     got = [send(piece, k) for piece, k in zip(pieces, TARGETS[0])]
     for steps in TARGETS[1:]:
-        pieces = attend_rest(steps, up, projected, out_weight, pieces[0].shape[2])
+        pieces = attend_rest(steps, up, normed, keyed, qkv_weight, out_weight, pieces[0].shape[2])
         got += [send(piece, k) for piece, k in zip(pieces, steps)]
     return unpack(sum(TARGETS, ()), got)
 

time: 72.8 us -> 72.2 us (level)
  waiting for transfers between devices: 17.4 us -> 15.8 us
  starting transfers between devices: 18 us -> 19.1 us
    ppermute x7, waiting for transfers between devices: 8.16 us -> 6.6 us  [send(): lax.ppermute(piece, 'frames', [(i, i ^ k) for i in range(devices)])]
    ppermute x7, starting transfers between devices: 10.3 us -> 11.4 us  [send(): lax.ppermute(piece, 'frames', [(i, i ^ k) for i in range(devices)])]
    pallas_call x2, Pallas kernels: 4.24 us -> 4.97 us  [attend_rest(): pl.pallas_call(functools.partial(attend_rest_kernel, steps), out_shape=(p...]
  transfers between devices with their start and end apart: 8 -> 8, of which waited for: 5 -> 3; matrix products, arithmetic and copies ran while one was open for 0% -> 0% of each run, Pallas kernels for 6% -> 7%
where the time goes in v4:
time: 72.2 us; the launch traced here: 71.9 us
  blocking collectives  21.4 us (30%)
  starting transfers between devices  19.1 us (26%)
  waiting for transfers between devices  15.8 us (22%)
  Pallas kernels  13.7 us (19%)
  local copies, waits for them, and re-layouts  1.9 us (3%)
    all_to_all x1, blocking collectives, per_device(): block = lax.all_to_all(sent, 'frames', 0, 0)  21.4 us
    ppermute x7, starting transfers between devices, send(): lax.ppermute(piece, 'frames', [(i, i ^ k) for i in range(devices)])  11.4 us
    all_to_all x1, waiting for transfers between devices, per_device(): stats = lax.all_to_all(copies, ('rows', 'frames'), 0, 0)  9.21 us
    all_to_all x1, starting transfers between devices, per_device(): stats = lax.all_to_all(copies, ('rows', 'frames'), 0, 0)  7.66 us
    ppermute x7, waiting for transfers between devices, send(): lax.ppermute(piece, 'frames', [(i, i ^ k) for i in range(devices)])  6.6 us
    pallas_call x2, Pallas kernels, attend_rest(): pl.pallas_call(functools.partial(attend_rest_kernel, steps), out_shape=(p...  4.97 us
    pallas_call x1, Pallas kernels, attend_first(): pl.pallas_call(functools.partial(attend_first_kernel, steps, count, 4), o...  3.48 us
    pallas_call x1, Pallas kernels, upsample(): pl.pallas_call(functools.partial(upsample_kernel, share), out_shape=(jax....  2.54 us
  transfers between devices with their start and end apart: 8, of which 3 were waited for; matrix products, arithmetic and copies ran while one was open for 0% of the time, Pallas kernels for 7%

profile of v4, /device:TPU:0, one launch (start us, length us, event | category | flops | bytes accessed | tf_op | source)
XLA Modules:
  0.0 71.9 jit_solution(4551154636786443045)
XLA Ops:
  0.0 1.2 %copy-done.1 = bf16[16,104,256]{2,1,0:T(8,128)(2,1)S(1)} copy-done((bf16[16,104,256]{2,1,0:T(8,128)(2,1)S(1)}, bf16[16,104,256]{2,1,0:T(8,128)(2,1)}, u32[]{:S(2)}) %copy-start.1) | copy-done | bytes 851992
  1.2 0.7 copy-done.4
  1.9 0.4 pack_latent.1
  2.3 0.0 copy-start.5
  2.3 0.0 copy-start
  2.3 0.0 copy-start.2
  2.4 21.4 %all_to_all.16.block_ref = bf16[8,240,256]{2,1,0:T(8,128)(2,1)S(1)} all-to-all(bf16[8,240,256]{2,1,0:T(8,128)(2,1)S(1)} %pack_latent.1), channel_id=1, replica_groups=mesh['rows'=16,'frames'=8] {'frames'}, dimensions={0} | all-to-all | bytes 1966080 | tf_op jit(solution)/shard_map/all_to_all | solution.py:345
  23.8 2.5 %upsample.1 = (bf16[13,2,128,256]{3,2,1,0:T(8,128)(2,1)S(1)}, f32[128,128]{1,0:T(8,128)}) custom-call(bf16[8,240,256]{2,1,0:T(8,128)(2,1)S(1)} %all_to_all.16.block_ref, bf16[4,256,256]{2,1,0:T(8,128)(2,1)S(1)} %copy-done.3), custom_call_target="tpu_custom_call" | custom-call | tf_op jit(solution)/shard_map/upsample/pallas_call | solution.py:134
  26.3 7.7 %all-to-all-start.1 = ((f32[128,1,128]{2,1,0:T(1,128)}), f32[128,1,128]{2,1,0:T(1,128)S(1)}, u32[]{:S(2)}, u32[]{:S(2)}) async-start(f32[128,1,128]{2,1,0:T(1,128)} %bitcast.1), calls=%async_computation.1 | async-start | bytes 131072 | tf_op jit(solution)/shard_map/all_to_all | solution.py:347
  34.0 9.2 %all-to-all-done.1 = f32[128,1,128]{2,1,0:T(1,128)S(1)} async-done(((f32[128,1,128]{2,1,0:T(1,128)}), f32[128,1,128]{2,1,0:T(1,128)S(1)}, u32[]{:S(2)}, u32[]{:S(2)}) %all-to-all-start.1) | async-done | bytes 65568 | tf_op jit(solution)/shard_map/all_to_all | solution.py:347
  43.2 3.5 %attend_first.1 = (bf16[13,2,16,256]{3,2,1,0:T(8,128)(2,1)S(1)}, bf16[13,2,16,256]{3,2,1,0:T(8,128)(2,1)S(1)}, bf16[3328,256]{1,0:T(8,128)(2,1)S(1)}, bf16[3328,512]{1,0:T(8,128)(2,1)S(1)}) custom-call(bf16[13,2,128,256]{3,2,1,0:T(8,128)(2,1)S(1)} %get-tuple-element.17.up_ref, f32[128,128]{1,0:T(8,128)S(1)} %bitcast.4, bf16[1,256]{1,0:T(2,128)(2,1)S(1)} %reshape.5.gain_ref, ...), custom_call_target="tpu_custom_call" | custom-call | flops 981467136 | bytes 851968 | tf_op jit(solution)/shard_map/attend_first/pallas_call | solution.py:266
  46.7 0.5 collective-permute-start
  47.2 1.5 %collective-permute-start.1 = (bf16[13,2,16,256]{3,2,1,0:T(8,128)(2,1)S(1)}, bf16[13,2,16,256]{3,2,1,0:T(8,128)(2,1)S(1)}, u32[]{:S(2)}, u32[]{:S(2)}) collective-permute-start(bf16[13,2,16,256]{3,2,1,0:T(8,128)(2,1)S(1)} %get-tuple-element.20), channel_id=1, source_target_pairs={{0,2},{1,3},{2,0},{3,1},{4,6},{5,7},{6,4},{7,5},{8,10},{9,11},{10,... | collective-permute-start | bytes 638984 | tf_op jit(solution)/shard_map/ppermute | solution.py:350
  48.7 2.5 %attend_rest.2 = (bf16[13,2,16,256]{3,2,1,0:T(8,128)(2,1)S(1)}, bf16[13,2,16,256]{3,2,1,0:T(8,128)(2,1)S(1)}, bf16[13,2,16,256]{3,2,1,0:T(8,128)(2,1)S(1)}) custom-call(bf16[13,2,128,256]{3,2,1,0:T(8,128)(2,1)S(1)} %get-tuple-element.17.up_ref, bf16[3328,256]{1,0:T(8,128)(2,1)S(1)} %get-tuple-element.21.normed_ref, ...), custom_call_target="tpu_custom_call" | custom-call | flops 1472200704 | bytes 1277952 | tf_op jit(solution)/shard_map/attend_rest/pallas_call | solution.py:284
  51.2 3.2 %collective-permute-start.2 = (bf16[13,2,16,256]{3,2,1,0:T(8,128)(2,1)S(1)}, bf16[13,2,16,256]{3,2,1,0:T(8,128)(2,1)S(1)}, u32[]{:S(2)}, u32[]{:S(2)}) collective-permute-start(bf16[13,2,16,256]{3,2,1,0:T(8,128)(2,1)S(1)} %get-tuple-element.23), channel_id=1, source_target_pairs={{0,6},{1,7},{2,4},{3,5},{4,2},{5,3},{6,0},{7,1},{8,14},{9,15},{10,... | collective-permute-start | bytes 638984 | tf_op jit(solution)/shard_map/ppermute | solution.py:350
  54.4 0.8 %collective-permute-start.3 = (bf16[13,2,16,256]{3,2,1,0:T(8,128)(2,1)S(1)}, bf16[13,2,16,256]{3,2,1,0:T(8,128)(2,1)S(1)}, u32[]{:S(2)}, u32[]{:S(2)}) collective-permute-start(bf16[13,2,16,256]{3,2,1,0:T(8,128)(2,1)S(1)} %get-tuple-element.24), channel_id=1, source_target_pairs={{0,7},{1,6},{2,5},{3,4},{4,3},{5,2},{6,1},{7,0},{8,15},{9,14},{10,... | collective-permute-start | bytes 638984 | tf_op jit(solution)/shard_map/ppermute | solution.py:350
  55.2 1.3 %collective-permute-start.4 = (bf16[13,2,16,256]{3,2,1,0:T(8,128)(2,1)S(1)}, bf16[13,2,16,256]{3,2,1,0:T(8,128)(2,1)S(1)}, u32[]{:S(2)}, u32[]{:S(2)}) collective-permute-start(bf16[13,2,16,256]{3,2,1,0:T(8,128)(2,1)S(1)} %get-tuple-element.25), channel_id=1, source_target_pairs={{0,5},{1,4},{2,7},{3,6},{4,1},{5,0},{6,3},{7,2},{8,13},{9,12},{10,... | collective-permute-start | bytes 638984 | tf_op jit(solution)/shard_map/ppermute | solution.py:350
  56.5 2.5 %attend_rest.3 = (bf16[13,2,16,256]{3,2,1,0:T(8,128)(2,1)S(1)}, bf16[13,2,16,256]{3,2,1,0:T(8,128)(2,1)S(1)}, bf16[13,2,16,256]{3,2,1,0:T(8,128)(2,1)S(1)}) custom-call(bf16[13,2,128,256]{3,2,1,0:T(8,128)(2,1)S(1)} %get-tuple-element.17.up_ref, bf16[3328,256]{1,0:T(8,128)(2,1)S(1)} %get-tuple-element.21.normed_ref, ...), custom_call_target="tpu_custom_call" | custom-call | flops 1472200704 | bytes 1277952 | tf_op jit(solution)/shard_map/attend_rest/pallas_call | solution.py:284
  59.0 0.0 collective-permute-done.refs_0_
  59.0 1.6 %collective-permute-start.5 = (bf16[13,2,16,256]{3,2,1,0:T(8,128)(2,1)S(1)}, bf16[13,2,16,256]{3,2,1,0:T(8,128)(2,1)S(1)}, u32[]{:S(2)}, u32[]{:S(2)}) collective-permute-start(bf16[13,2,16,256]{3,2,1,0:T(8,128)(2,1)S(1)} %get-tuple-element.26), channel_id=1, source_target_pairs={{0,1},{1,0},{2,3},{3,2},{4,5},{5,4},{6,7},{7,6},{8,9},{9,8},{10,11... | collective-permute-start | bytes 638984 | tf_op jit(solution)/shard_map/ppermute | solution.py:350
  60.6 2.5 %collective-permute-start.6 = (bf16[13,2,16,256]{3,2,1,0:T(8,128)(2,1)S(1)}, bf16[13,2,16,256]{3,2,1,0:T(8,128)(2,1)S(1)}, u32[]{:S(2)}, u32[]{:S(2)}) collective-permute-start(bf16[13,2,16,256]{3,2,1,0:T(8,128)(2,1)S(1)} %get-tuple-element.27), channel_id=1, source_target_pairs={{0,3},{1,2},{2,1},{3,0},{4,7},{5,6},{6,5},{7,4},{8,11},{9,10},{10,... | collective-permute-start | bytes 638984 | tf_op jit(solution)/shard_map/ppermute | solution.py:350
  63.1 3.0 %collective-permute-done.3.refs_3_ = bf16[13,2,16,256]{3,2,1,0:T(8,128)(2,1)S(1)} collective-permute-done((bf16[13,2,16,256]{3,2,1,0:T(8,128)(2,1)S(1)}, bf16[13,2,16,256]{3,2,1,0:T(8,128)(2,1)S(1)}, u32[]{:S(2)}, u32[]{:S(2)}) %collective-permute-start.3) | collective-permute-done | bytes 213024 | tf_op jit(solution)/shard_map/ppermute | solution.py:350
  66.1 3.6 %collective-permute-done.4.refs_4_ = bf16[13,2,16,256]{3,2,1,0:T(8,128)(2,1)S(1)} collective-permute-done((bf16[13,2,16,256]{3,2,1,0:T(8,128)(2,1)S(1)}, bf16[13,2,16,256]{3,2,1,0:T(8,128)(2,1)S(1)}, u32[]{:S(2)}, u32[]{:S(2)}) %collective-permute-start.4) | collective-permute-done | bytes 213024 | tf_op jit(solution)/shard_map/ppermute | solution.py:350
  69.7 2.2 %unpack_output.1 = bf16[32,104,256]{2,1,0:T(8,128)(2,1)} custom-call(bf16[13,2,16,256]{3,2,1,0:T(8,128)(2,1)S(1)} %collective-permute-done.refs_0_, bf16[13,2,16,256]{3,2,1,0:T(8,128)(2,1)S(1)} %collective-permute-done.1.refs_1_, bf16[13,2,16,256]{3,2,1,0:T(8,128)(2,1)S(1)} %collective-permute-done.2.refs_2_, ...), custom_call_target="tpu_custom_call" | custom-call | tf_op jit(solution)/shard_map/unpack_output/pallas_call | solution.py:323
  (12 shorter events, 0.0 us)
Async XLA Ops:
  0.0 1.2 %copy-start.1 = (bf16[16,104,256]{2,1,0:T(8,128)(2,1)S(1)}, bf16[16,104,256]{2,1,0:T(8,128)(2,1)}, u32[]{:S(2)}) copy-start(bf16[16,104,256]{2,1,0:T(8,128)(2,1)} %latent_ref.1) | copy-start | bytes 2555908
  1.2 0.7 copy-start.4
  1.9 21.9 %copy-start.3 = (bf16[4,256,256]{2,1,0:T(8,128)(2,1)S(1)}, bf16[4,256,256]{2,1,0:T(8,128)(2,1)}, u32[]{:S(2)}) copy-start(bf16[4,256,256]{2,1,0:T(8,128)(2,1)} %conv_ref.1) | copy-start | bytes 1572868
  2.3 31.7 %copy-start.5 = (bf16[256]{0:T(256)(128)(2,1)S(1)}, bf16[256]{0:T(256)(128)(2,1)}, u32[]{:S(2)}) copy-start(bf16[256]{0:T(256)(128)(2,1)} %param.8) | copy-start | bytes 1540
  2.3 40.9 %copy-start = (bf16[256,768]{1,0:T(8,128)(2,1)S(1)}, bf16[256,768]{1,0:T(8,128)(2,1)}, u32[]{:S(2)}) copy-start(bf16[256,768]{1,0:T(8,128)(2,1)} %qkv_ref.5) | copy-start | bytes 1179652
  2.3 40.9 %copy-start.2 = (bf16[256,256]{1,0:T(8,128)(2,1)S(1)}, bf16[256,256]{1,0:T(8,128)(2,1)}, u32[]{:S(2)}) copy-start(bf16[256,256]{1,0:T(8,128)(2,1)} %out_weight_ref.5) | copy-start | bytes 393220
  26.3 16.9 %all-to-all-start.1 = ((f32[128,1,128]{2,1,0:T(1,128)}), f32[128,1,128]{2,1,0:T(1,128)S(1)}, u32[]{:S(2)}, u32[]{:S(2)}) async-start(f32[128,1,128]{2,1,0:T(1,128)} %bitcast.1), calls=%async_computation.1 | async-start | bytes 131072 | tf_op jit(solution)/shard_map/all_to_all | solution.py:347
  46.7 12.3 %collective-permute-start = (bf16[13,2,16,256]{3,2,1,0:T(8,128)(2,1)S(1)}, bf16[13,2,16,256]{3,2,1,0:T(8,128)(2,1)S(1)}, u32[]{:S(2)}, u32[]{:S(2)}) collective-permute-start(bf16[13,2,16,256]{3,2,1,0:T(8,128)(2,1)S(1)} %get-tuple-element.19), channel_id=1, source_target_pairs={{0,4},{1,5},{2,6},{3,7},{4,0},{5,1},{6,2},{7,3},{8,12},{9,13},{10,... | collective-permute-start | bytes 638984 | tf_op jit(solution)/shard_map/ppermute | solution.py:350
  47.2 13.4 %collective-permute-start.1 = (bf16[13,2,16,256]{3,2,1,0:T(8,128)(2,1)S(1)}, bf16[13,2,16,256]{3,2,1,0:T(8,128)(2,1)S(1)}, u32[]{:S(2)}, u32[]{:S(2)}) collective-permute-start(bf16[13,2,16,256]{3,2,1,0:T(8,128)(2,1)S(1)} %get-tuple-element.20), channel_id=1, source_target_pairs={{0,2},{1,3},{2,0},{3,1},{4,6},{5,7},{6,4},{7,5},{8,10},{9,11},{10,... | collective-permute-start | bytes 638984 | tf_op jit(solution)/shard_map/ppermute | solution.py:350
  51.2 11.9 %collective-permute-start.2 = (bf16[13,2,16,256]{3,2,1,0:T(8,128)(2,1)S(1)}, bf16[13,2,16,256]{3,2,1,0:T(8,128)(2,1)S(1)}, u32[]{:S(2)}, u32[]{:S(2)}) collective-permute-start(bf16[13,2,16,256]{3,2,1,0:T(8,128)(2,1)S(1)} %get-tuple-element.23), channel_id=1, source_target_pairs={{0,6},{1,7},{2,4},{3,5},{4,2},{5,3},{6,0},{7,1},{8,14},{9,15},{10,... | collective-permute-start | bytes 638984 | tf_op jit(solution)/shard_map/ppermute | solution.py:350
  54.4 11.7 %collective-permute-start.3 = (bf16[13,2,16,256]{3,2,1,0:T(8,128)(2,1)S(1)}, bf16[13,2,16,256]{3,2,1,0:T(8,128)(2,1)S(1)}, u32[]{:S(2)}, u32[]{:S(2)}) collective-permute-start(bf16[13,2,16,256]{3,2,1,0:T(8,128)(2,1)S(1)} %get-tuple-element.24), channel_id=1, source_target_pairs={{0,7},{1,6},{2,5},{3,4},{4,3},{5,2},{6,1},{7,0},{8,15},{9,14},{10,... | collective-permute-start | bytes 638984 | tf_op jit(solution)/shard_map/ppermute | solution.py:350
  55.2 14.5 %collective-permute-start.4 = (bf16[13,2,16,256]{3,2,1,0:T(8,128)(2,1)S(1)}, bf16[13,2,16,256]{3,2,1,0:T(8,128)(2,1)S(1)}, u32[]{:S(2)}, u32[]{:S(2)}) collective-permute-start(bf16[13,2,16,256]{3,2,1,0:T(8,128)(2,1)S(1)} %get-tuple-element.25), channel_id=1, source_target_pairs={{0,5},{1,4},{2,7},{3,6},{4,1},{5,0},{6,3},{7,2},{8,13},{9,12},{10,... | collective-permute-start | bytes 638984 | tf_op jit(solution)/shard_map/ppermute | solution.py:350
  59.0 10.7 %collective-permute-start.5 = (bf16[13,2,16,256]{3,2,1,0:T(8,128)(2,1)S(1)}, bf16[13,2,16,256]{3,2,1,0:T(8,128)(2,1)S(1)}, u32[]{:S(2)}, u32[]{:S(2)}) collective-permute-start(bf16[13,2,16,256]{3,2,1,0:T(8,128)(2,1)S(1)} %get-tuple-element.26), channel_id=1, source_target_pairs={{0,1},{1,0},{2,3},{3,2},{4,5},{5,4},{6,7},{7,6},{8,9},{9,8},{10,11... | collective-permute-start | bytes 638984 | tf_op jit(solution)/shard_map/ppermute | solution.py:350
  60.6 9.1 %collective-permute-start.6 = (bf16[13,2,16,256]{3,2,1,0:T(8,128)(2,1)S(1)}, bf16[13,2,16,256]{3,2,1,0:T(8,128)(2,1)S(1)}, u32[]{:S(2)}, u32[]{:S(2)}) collective-permute-start(bf16[13,2,16,256]{3,2,1,0:T(8,128)(2,1)S(1)} %get-tuple-element.27), channel_id=1, source_target_pairs={{0,3},{1,2},{2,1},{3,0},{4,7},{5,6},{6,5},{7,4},{8,11},{9,10},{10,... | collective-permute-start | bytes 638984 | tf_op jit(solution)/shard_map/ppermute | solution.py:350

commit v5 on v4

--- a/solution.py
+++ b/solution.py
@@ -22,18 +22,23 @@
     return pltpu.CompilerParams(vmem_limit_bytes=mib * 1024 * 1024)
 
 
+def pitch_of(pixels):
+    return pixels + 1 - pixels % 2
+
+
 def pack_kernel(latent_ref, embed_ref, out_ref, wide, embed_wide):
     frames, pixels, _ = latent_ref.shape
     devices = out_ref.shape[0]
     share = pixels // devices
+    pitch = pitch_of(pixels)
     for half in range(wide.shape[0]):
         lanes = slice(half * LANES, (half + 1) * LANES)
         for f in range(frames):
-            wide[half, f * pixels : (f + 1) * pixels, :] = latent_ref[f, :, lanes].astype(F32)
-        embed_wide[half] = embed_ref[:, lanes].astype(F32)
+            wide[half, f * pitch : f * pitch + pixels, :] = latent_ref[f, :, lanes].astype(F32)
+        embed_wide[half, 0 : 2 * frames] = embed_ref[:, lanes].astype(F32)
         for p in range(pixels):
             d, j = divmod(p, share)
-            rows = wide[half, pl.ds(p, frames, stride=pixels), :].astype(BF16)
+            rows = wide[half, pl.ds(p, frames, stride=pitch), :].astype(BF16)
             out_ref[d, j * frames : (j + 1) * frames, lanes] = rows
         for parity in range(2):
             rows = embed_wide[half, pl.ds(parity, frames, stride=2), :].astype(BF16)
@@ -49,8 +54,8 @@
         pack_kernel,
         out_shape=jax.ShapeDtypeStruct((devices, rows, channels), BF16),
         scratch_shapes=[
-            pltpu.VMEM((channels // LANES, frames * pixels, LANES), F32),
-            pltpu.VMEM((channels // LANES, 2 * frames, LANES), F32),
+            pltpu.VMEM((channels // LANES, (frames + 1) * pitch_of(pixels), LANES), F32),
+            pltpu.VMEM((channels // LANES, 2 * frames + 8, LANES), F32),
         ],
         compiler_params=params(24),
         name="pack_latent",
@@ -294,22 +299,25 @@
 def unpack_kernel(steps, *refs):
     *block_refs, out_hbm, held, wide, sems = refs
     frames, pixels, _ = held.shape
+    share, _, part, _ = block_refs[0].shape
     pieces = sems.shape[1]
     step = frames // pieces
+    pitch = pitch_of(pixels)
+    me = lax.axis_index("frames")
     copies = []
-    share, _, part, _ = block_refs[0].shape
-    me = lax.axis_index("frames")
     for half in range(wide.shape[0]):
         lanes = slice(half * LANES, (half + 1) * LANES)
         for k, block_ref in zip(steps, block_refs):
             for j in range(share):
                 for parity in range(2):
-                    start = parity * pixels + j + (me ^ k) * share
+                    start = parity * part * pitch + j + (me ^ k) * share
                     rows = block_ref[j, parity, :, lanes].astype(F32)
-                    wide[half, pl.ds(start, part, stride=2 * pixels), :] = rows
+                    wide[half, pl.ds(start, part, stride=pitch), :] = rows
         for i in range(pieces):
             for f in range(i * step, (i + 1) * step):
-                held[f, :, lanes] = wide[half, f * pixels : (f + 1) * pixels, :].astype(BF16)
+                m, parity = divmod(f, 2)
+                first = (parity * part + m) * pitch
+                held[f, :, lanes] = wide[half, first : first + pixels, :].astype(BF16)
             span = (pl.ds(i * step, step), slice(None), pl.ds(half * LANES, LANES))
             copies.append(pltpu.make_async_copy(held.at[span], out_hbm.at[span], sems.at[half, i]))
             copies[-1].start()
@@ -326,7 +334,7 @@
         out_specs=pl.BlockSpec(memory_space=pltpu.HBM),
         scratch_shapes=[
             pltpu.VMEM((frames, pixels, channels), BF16),
-            pltpu.VMEM((channels // LANES, frames * pixels, LANES), F32),
+            pltpu.VMEM((channels // LANES, (frames + 1) * pitch_of(pixels), LANES), F32),
             pltpu.SemaphoreType.DMA((channels // LANES, 4)),
         ],
         compiler_params=params(24),

time: 72.2 us -> 71.2 us (0.986)
  Pallas kernels: 13.7 us -> 12.7 us
    pallas_call x1, Pallas kernels: 2.22 us -> 1.4 us  [unpack(): pl.pallas_call(functools.partial(unpack_kernel, steps), out_shape=jax.Sha...]
where the time goes in v5:
time: 71.2 us; the launch traced here: 70.9 us
  blocking collectives  21.4 us (30%)
  starting transfers between devices  19.1 us (27%)
  waiting for transfers between devices  15.8 us (22%)
  Pallas kernels  12.7 us (18%)
  local copies, waits for them, and re-layouts  1.9 us (3%)
    all_to_all x1, blocking collectives, per_device(): block = lax.all_to_all(sent, 'frames', 0, 0)  21.4 us
    ppermute x7, starting transfers between devices, send(): lax.ppermute(piece, 'frames', [(i, i ^ k) for i in range(devices)])  11.4 us
    all_to_all x1, waiting for transfers between devices, per_device(): stats = lax.all_to_all(copies, ('rows', 'frames'), 0, 0)  9.21 us
    all_to_all x1, starting transfers between devices, per_device(): stats = lax.all_to_all(copies, ('rows', 'frames'), 0, 0)  7.66 us
    ppermute x7, waiting for transfers between devices, send(): lax.ppermute(piece, 'frames', [(i, i ^ k) for i in range(devices)])  6.59 us
    pallas_call x2, Pallas kernels, attend_rest(): pl.pallas_call(functools.partial(attend_rest_kernel, steps), out_shape=(p...  4.97 us
    pallas_call x1, Pallas kernels, attend_first(): pl.pallas_call(functools.partial(attend_first_kernel, steps, count, 4), o...  3.49 us
    pallas_call x1, Pallas kernels, upsample(): pl.pallas_call(functools.partial(upsample_kernel, share), out_shape=(jax....  2.54 us
  transfers between devices with their start and end apart: 8, of which 3 were waited for; matrix products, arithmetic and copies ran while one was open for 0% of the time, Pallas kernels for 7%

profile of v5, /device:TPU:0, one launch (start us, length us, event | category | flops | bytes accessed | tf_op | source)
XLA Modules:
  0.0 70.9 jit_solution(8418183706830379064)
XLA Ops:
  0.0 1.2 %copy-done.1 = bf16[16,104,256]{2,1,0:T(8,128)(2,1)S(1)} copy-done((bf16[16,104,256]{2,1,0:T(8,128)(2,1)S(1)}, bf16[16,104,256]{2,1,0:T(8,128)(2,1)}, u32[]{:S(2)}) %copy-start.1) | copy-done | bytes 851992
  1.2 0.7 %copy-done.4 = bf16[32,256]{1,0:T(8,128)(2,1)S(1)} copy-done((bf16[32,256]{1,0:T(8,128)(2,1)S(1)}, bf16[32,256]{1,0:T(8,128)(2,1)}, u32[]{:S(2)}) %copy-start.4) | copy-done | bytes 16408
  1.9 0.3 pack_latent.1
  2.2 0.0 copy-start.5
  2.2 0.0 copy-start
  2.2 0.0 copy-start.2
  2.2 21.4 %all_to_all.16.block_ref = bf16[8,240,256]{2,1,0:T(8,128)(2,1)S(1)} all-to-all(bf16[8,240,256]{2,1,0:T(8,128)(2,1)S(1)} %pack_latent.1), channel_id=1, replica_groups=mesh['rows'=16,'frames'=8] {'frames'}, dimensions={0} | all-to-all | bytes 1966080 | tf_op jit(solution)/shard_map/all_to_all | solution.py:353
  23.6 2.5 %upsample.1 = (bf16[13,2,128,256]{3,2,1,0:T(8,128)(2,1)S(1)}, f32[128,128]{1,0:T(8,128)}) custom-call(bf16[8,240,256]{2,1,0:T(8,128)(2,1)S(1)} %all_to_all.16.block_ref, bf16[4,256,256]{2,1,0:T(8,128)(2,1)S(1)} %copy-done.3), custom_call_target="tpu_custom_call" | custom-call | tf_op jit(solution)/shard_map/upsample/pallas_call | solution.py:139
  26.2 7.7 %all-to-all-start.1 = ((f32[128,1,128]{2,1,0:T(1,128)}), f32[128,1,128]{2,1,0:T(1,128)S(1)}, u32[]{:S(2)}, u32[]{:S(2)}) async-start(f32[128,1,128]{2,1,0:T(1,128)} %bitcast.1), calls=%async_computation.1 | async-start | bytes 131072 | tf_op jit(solution)/shard_map/all_to_all | solution.py:355
  33.9 9.2 %all-to-all-done.1 = f32[128,1,128]{2,1,0:T(1,128)S(1)} async-done(((f32[128,1,128]{2,1,0:T(1,128)}), f32[128,1,128]{2,1,0:T(1,128)S(1)}, u32[]{:S(2)}, u32[]{:S(2)}) %all-to-all-start.1) | async-done | bytes 65568 | tf_op jit(solution)/shard_map/all_to_all | solution.py:355
  43.1 3.5 %attend_first.1 = (bf16[13,2,16,256]{3,2,1,0:T(8,128)(2,1)S(1)}, bf16[13,2,16,256]{3,2,1,0:T(8,128)(2,1)S(1)}, bf16[3328,256]{1,0:T(8,128)(2,1)S(1)}, bf16[3328,512]{1,0:T(8,128)(2,1)S(1)}) custom-call(bf16[13,2,128,256]{3,2,1,0:T(8,128)(2,1)S(1)} %get-tuple-element.17.up_ref, f32[128,128]{1,0:T(8,128)S(1)} %bitcast.4, bf16[1,256]{1,0:T(2,128)(2,1)S(1)} %reshape.5.gain_ref, ...), custom_call_target="tpu_custom_call" | custom-call | flops 981467136 | bytes 851968 | tf_op jit(solution)/shard_map/attend_first/pallas_call | solution.py:271
  46.6 0.4 collective-permute-start
  47.0 1.5 %collective-permute-start.1 = (bf16[13,2,16,256]{3,2,1,0:T(8,128)(2,1)S(1)}, bf16[13,2,16,256]{3,2,1,0:T(8,128)(2,1)S(1)}, u32[]{:S(2)}, u32[]{:S(2)}) collective-permute-start(bf16[13,2,16,256]{3,2,1,0:T(8,128)(2,1)S(1)} %get-tuple-element.20), channel_id=1, source_target_pairs={{0,2},{1,3},{2,0},{3,1},{4,6},{5,7},{6,4},{7,5},{8,10},{9,11},{10,... | collective-permute-start | bytes 638984 | tf_op jit(solution)/shard_map/ppermute | solution.py:358
  48.5 2.5 %attend_rest.2 = (bf16[13,2,16,256]{3,2,1,0:T(8,128)(2,1)S(1)}, bf16[13,2,16,256]{3,2,1,0:T(8,128)(2,1)S(1)}, bf16[13,2,16,256]{3,2,1,0:T(8,128)(2,1)S(1)}) custom-call(bf16[13,2,128,256]{3,2,1,0:T(8,128)(2,1)S(1)} %get-tuple-element.17.up_ref, bf16[3328,256]{1,0:T(8,128)(2,1)S(1)} %get-tuple-element.21.normed_ref, ...), custom_call_target="tpu_custom_call" | custom-call | flops 1472200704 | bytes 1277952 | tf_op jit(solution)/shard_map/attend_rest/pallas_call | solution.py:289
  51.0 3.2 %collective-permute-start.2 = (bf16[13,2,16,256]{3,2,1,0:T(8,128)(2,1)S(1)}, bf16[13,2,16,256]{3,2,1,0:T(8,128)(2,1)S(1)}, u32[]{:S(2)}, u32[]{:S(2)}) collective-permute-start(bf16[13,2,16,256]{3,2,1,0:T(8,128)(2,1)S(1)} %get-tuple-element.23), channel_id=1, source_target_pairs={{0,6},{1,7},{2,4},{3,5},{4,2},{5,3},{6,0},{7,1},{8,14},{9,15},{10,... | collective-permute-start | bytes 638984 | tf_op jit(solution)/shard_map/ppermute | solution.py:358
  54.2 0.8 %collective-permute-start.3 = (bf16[13,2,16,256]{3,2,1,0:T(8,128)(2,1)S(1)}, bf16[13,2,16,256]{3,2,1,0:T(8,128)(2,1)S(1)}, u32[]{:S(2)}, u32[]{:S(2)}) collective-permute-start(bf16[13,2,16,256]{3,2,1,0:T(8,128)(2,1)S(1)} %get-tuple-element.24), channel_id=1, source_target_pairs={{0,7},{1,6},{2,5},{3,4},{4,3},{5,2},{6,1},{7,0},{8,15},{9,14},{10,... | collective-permute-start | bytes 638984 | tf_op jit(solution)/shard_map/ppermute | solution.py:358
  55.0 1.3 %collective-permute-start.4 = (bf16[13,2,16,256]{3,2,1,0:T(8,128)(2,1)S(1)}, bf16[13,2,16,256]{3,2,1,0:T(8,128)(2,1)S(1)}, u32[]{:S(2)}, u32[]{:S(2)}) collective-permute-start(bf16[13,2,16,256]{3,2,1,0:T(8,128)(2,1)S(1)} %get-tuple-element.25), channel_id=1, source_target_pairs={{0,5},{1,4},{2,7},{3,6},{4,1},{5,0},{6,3},{7,2},{8,13},{9,12},{10,... | collective-permute-start | bytes 638984 | tf_op jit(solution)/shard_map/ppermute | solution.py:358
  56.3 2.5 %attend_rest.3 = (bf16[13,2,16,256]{3,2,1,0:T(8,128)(2,1)S(1)}, bf16[13,2,16,256]{3,2,1,0:T(8,128)(2,1)S(1)}, bf16[13,2,16,256]{3,2,1,0:T(8,128)(2,1)S(1)}) custom-call(bf16[13,2,128,256]{3,2,1,0:T(8,128)(2,1)S(1)} %get-tuple-element.17.up_ref, bf16[3328,256]{1,0:T(8,128)(2,1)S(1)} %get-tuple-element.21.normed_ref, ...), custom_call_target="tpu_custom_call" | custom-call | flops 1472200704 | bytes 1277952 | tf_op jit(solution)/shard_map/attend_rest/pallas_call | solution.py:289
  58.8 0.0 collective-permute-done.refs_0_
  58.8 1.6 %collective-permute-start.5 = (bf16[13,2,16,256]{3,2,1,0:T(8,128)(2,1)S(1)}, bf16[13,2,16,256]{3,2,1,0:T(8,128)(2,1)S(1)}, u32[]{:S(2)}, u32[]{:S(2)}) collective-permute-start(bf16[13,2,16,256]{3,2,1,0:T(8,128)(2,1)S(1)} %get-tuple-element.26), channel_id=1, source_target_pairs={{0,1},{1,0},{2,3},{3,2},{4,5},{5,4},{6,7},{7,6},{8,9},{9,8},{10,11... | collective-permute-start | bytes 638984 | tf_op jit(solution)/shard_map/ppermute | solution.py:358
  60.5 2.5 %collective-permute-start.6 = (bf16[13,2,16,256]{3,2,1,0:T(8,128)(2,1)S(1)}, bf16[13,2,16,256]{3,2,1,0:T(8,128)(2,1)S(1)}, u32[]{:S(2)}, u32[]{:S(2)}) collective-permute-start(bf16[13,2,16,256]{3,2,1,0:T(8,128)(2,1)S(1)} %get-tuple-element.27), channel_id=1, source_target_pairs={{0,3},{1,2},{2,1},{3,0},{4,7},{5,6},{6,5},{7,4},{8,11},{9,10},{10,... | collective-permute-start | bytes 638984 | tf_op jit(solution)/shard_map/ppermute | solution.py:358
  63.0 2.9 %collective-permute-done.3.refs_3_ = bf16[13,2,16,256]{3,2,1,0:T(8,128)(2,1)S(1)} collective-permute-done((bf16[13,2,16,256]{3,2,1,0:T(8,128)(2,1)S(1)}, bf16[13,2,16,256]{3,2,1,0:T(8,128)(2,1)S(1)}, u32[]{:S(2)}, u32[]{:S(2)}) %collective-permute-start.3) | collective-permute-done | bytes 213024 | tf_op jit(solution)/shard_map/ppermute | solution.py:358
  65.9 3.6 %collective-permute-done.4.refs_4_ = bf16[13,2,16,256]{3,2,1,0:T(8,128)(2,1)S(1)} collective-permute-done((bf16[13,2,16,256]{3,2,1,0:T(8,128)(2,1)S(1)}, bf16[13,2,16,256]{3,2,1,0:T(8,128)(2,1)S(1)}, u32[]{:S(2)}, u32[]{:S(2)}) %collective-permute-start.4) | collective-permute-done | bytes 213024 | tf_op jit(solution)/shard_map/ppermute | solution.py:358
  69.6 1.4 %unpack_output.1 = bf16[32,104,256]{2,1,0:T(8,128)(2,1)} custom-call(bf16[13,2,16,256]{3,2,1,0:T(8,128)(2,1)S(1)} %collective-permute-done.refs_0_, bf16[13,2,16,256]{3,2,1,0:T(8,128)(2,1)S(1)} %collective-permute-done.1.refs_1_, bf16[13,2,16,256]{3,2,1,0:T(8,128)(2,1)S(1)} %collective-permute-done.2.refs_2_, ...), custom_call_target="tpu_custom_call" | custom-call | tf_op jit(solution)/shard_map/unpack_output/pallas_call | solution.py:331
  (12 shorter events, 0.0 us)
Async XLA Ops:
  0.0 1.2 %copy-start.1 = (bf16[16,104,256]{2,1,0:T(8,128)(2,1)S(1)}, bf16[16,104,256]{2,1,0:T(8,128)(2,1)}, u32[]{:S(2)}) copy-start(bf16[16,104,256]{2,1,0:T(8,128)(2,1)} %latent_ref.1) | copy-start | bytes 2555908
  1.2 0.7 %copy-start.4 = (bf16[32,256]{1,0:T(8,128)(2,1)S(1)}, bf16[32,256]{1,0:T(8,128)(2,1)}, u32[]{:S(2)}) copy-start(bf16[32,256]{1,0:T(8,128)(2,1)} %embed_ref.1) | copy-start | bytes 49156
  1.9 21.7 %copy-start.3 = (bf16[4,256,256]{2,1,0:T(8,128)(2,1)S(1)}, bf16[4,256,256]{2,1,0:T(8,128)(2,1)}, u32[]{:S(2)}) copy-start(bf16[4,256,256]{2,1,0:T(8,128)(2,1)} %conv_ref.1) | copy-start | bytes 1572868
  2.2 31.7 %copy-start.5 = (bf16[256]{0:T(256)(128)(2,1)S(1)}, bf16[256]{0:T(256)(128)(2,1)}, u32[]{:S(2)}) copy-start(bf16[256]{0:T(256)(128)(2,1)} %param.8) | copy-start | bytes 1540
  2.2 40.9 %copy-start = (bf16[256,768]{1,0:T(8,128)(2,1)S(1)}, bf16[256,768]{1,0:T(8,128)(2,1)}, u32[]{:S(2)}) copy-start(bf16[256,768]{1,0:T(8,128)(2,1)} %qkv_ref.5) | copy-start | bytes 1179652
  2.2 40.9 %copy-start.2 = (bf16[256,256]{1,0:T(8,128)(2,1)S(1)}, bf16[256,256]{1,0:T(8,128)(2,1)}, u32[]{:S(2)}) copy-start(bf16[256,256]{1,0:T(8,128)(2,1)} %out_weight_ref.5) | copy-start | bytes 393220
  26.2 16.9 %all-to-all-start.1 = ((f32[128,1,128]{2,1,0:T(1,128)}), f32[128,1,128]{2,1,0:T(1,128)S(1)}, u32[]{:S(2)}, u32[]{:S(2)}) async-start(f32[128,1,128]{2,1,0:T(1,128)} %bitcast.1), calls=%async_computation.1 | async-start | bytes 131072 | tf_op jit(solution)/shard_map/all_to_all | solution.py:355
  46.6 12.3 %collective-permute-start = (bf16[13,2,16,256]{3,2,1,0:T(8,128)(2,1)S(1)}, bf16[13,2,16,256]{3,2,1,0:T(8,128)(2,1)S(1)}, u32[]{:S(2)}, u32[]{:S(2)}) collective-permute-start(bf16[13,2,16,256]{3,2,1,0:T(8,128)(2,1)S(1)} %get-tuple-element.19), channel_id=1, source_target_pairs={{0,4},{1,5},{2,6},{3,7},{4,0},{5,1},{6,2},{7,3},{8,12},{9,13},{10,... | collective-permute-start | bytes 638984 | tf_op jit(solution)/shard_map/ppermute | solution.py:358
  47.0 13.5 %collective-permute-start.1 = (bf16[13,2,16,256]{3,2,1,0:T(8,128)(2,1)S(1)}, bf16[13,2,16,256]{3,2,1,0:T(8,128)(2,1)S(1)}, u32[]{:S(2)}, u32[]{:S(2)}) collective-permute-start(bf16[13,2,16,256]{3,2,1,0:T(8,128)(2,1)S(1)} %get-tuple-element.20), channel_id=1, source_target_pairs={{0,2},{1,3},{2,0},{3,1},{4,6},{5,7},{6,4},{7,5},{8,10},{9,11},{10,... | collective-permute-start | bytes 638984 | tf_op jit(solution)/shard_map/ppermute | solution.py:358
  51.0 11.9 %collective-permute-start.2 = (bf16[13,2,16,256]{3,2,1,0:T(8,128)(2,1)S(1)}, bf16[13,2,16,256]{3,2,1,0:T(8,128)(2,1)S(1)}, u32[]{:S(2)}, u32[]{:S(2)}) collective-permute-start(bf16[13,2,16,256]{3,2,1,0:T(8,128)(2,1)S(1)} %get-tuple-element.23), channel_id=1, source_target_pairs={{0,6},{1,7},{2,4},{3,5},{4,2},{5,3},{6,0},{7,1},{8,14},{9,15},{10,... | collective-permute-start | bytes 638984 | tf_op jit(solution)/shard_map/ppermute | solution.py:358
  54.2 11.7 %collective-permute-start.3 = (bf16[13,2,16,256]{3,2,1,0:T(8,128)(2,1)S(1)}, bf16[13,2,16,256]{3,2,1,0:T(8,128)(2,1)S(1)}, u32[]{:S(2)}, u32[]{:S(2)}) collective-permute-start(bf16[13,2,16,256]{3,2,1,0:T(8,128)(2,1)S(1)} %get-tuple-element.24), channel_id=1, source_target_pairs={{0,7},{1,6},{2,5},{3,4},{4,3},{5,2},{6,1},{7,0},{8,15},{9,14},{10,... | collective-permute-start | bytes 638984 | tf_op jit(solution)/shard_map/ppermute | solution.py:358
  55.0 14.5 %collective-permute-start.4 = (bf16[13,2,16,256]{3,2,1,0:T(8,128)(2,1)S(1)}, bf16[13,2,16,256]{3,2,1,0:T(8,128)(2,1)S(1)}, u32[]{:S(2)}, u32[]{:S(2)}) collective-permute-start(bf16[13,2,16,256]{3,2,1,0:T(8,128)(2,1)S(1)} %get-tuple-element.25), channel_id=1, source_target_pairs={{0,5},{1,4},{2,7},{3,6},{4,1},{5,0},{6,3},{7,2},{8,13},{9,12},{10,... | collective-permute-start | bytes 638984 | tf_op jit(solution)/shard_map/ppermute | solution.py:358
  58.8 10.7 %collective-permute-start.5 = (bf16[13,2,16,256]{3,2,1,0:T(8,128)(2,1)S(1)}, bf16[13,2,16,256]{3,2,1,0:T(8,128)(2,1)S(1)}, u32[]{:S(2)}, u32[]{:S(2)}) collective-permute-start(bf16[13,2,16,256]{3,2,1,0:T(8,128)(2,1)S(1)} %get-tuple-element.26), channel_id=1, source_target_pairs={{0,1},{1,0},{2,3},{3,2},{4,5},{5,4},{6,7},{7,6},{8,9},{9,8},{10,11... | collective-permute-start | bytes 638984 | tf_op jit(solution)/shard_map/ppermute | solution.py:358
  60.5 9.1 %collective-permute-start.6 = (bf16[13,2,16,256]{3,2,1,0:T(8,128)(2,1)S(1)}, bf16[13,2,16,256]{3,2,1,0:T(8,128)(2,1)S(1)}, u32[]{:S(2)}, u32[]{:S(2)}) collective-permute-start(bf16[13,2,16,256]{3,2,1,0:T(8,128)(2,1)S(1)} %get-tuple-element.27), channel_id=1, source_target_pairs={{0,3},{1,2},{2,1},{3,0},{4,7},{5,6},{6,5},{7,4},{8,11},{9,10},{10,... | collective-permute-start | bytes 638984 | tf_op jit(solution)/shard_map/ppermute | solution.py:358

commit v6 on v5

--- a/solution.py
+++ b/solution.py
@@ -342,7 +342,7 @@
     )(*blocks)
 
 
-TARGETS = ((4, 2), (6, 7, 5), (1, 3, 0))
+TARGETS = ((4, 2), (6, 7), (5, 1, 3, 0))
 
 
 def per_device(latent, conv_weight, norm_gain, frame_embed, qkv_weight, out_weight):

time: 71.2 us -> 71.1 us (level)
  starting transfers between devices: 19.1 us -> 17.4 us
  waiting for transfers between devices: 15.8 us -> 17.2 us
    ppermute x7, starting transfers between devices: 11.4 us -> 9.77 us  [send(): lax.ppermute(piece, 'frames', [(i, i ^ k) for i in range(devices)])]
    ppermute x7, waiting for transfers between devices: 6.59 us -> 7.98 us  [send(): lax.ppermute(piece, 'frames', [(i, i ^ k) for i in range(devices)])]
  transfers between devices with their start and end apart: 8 -> 8, of which waited for: 3 -> 5; matrix products, arithmetic and copies ran while one was open for 0% -> 0% of each run, Pallas kernels for 7% -> 7%
where the time goes in v6:
time: 71.1 us; the launch traced here: 70.8 us
  blocking collectives  21.4 us (30%)
  starting transfers between devices  17.4 us (24%)
  waiting for transfers between devices  17.2 us (24%)
  Pallas kernels  12.8 us (18%)
  local copies, waits for them, and re-layouts  1.9 us (3%)
    all_to_all x1, blocking collectives, per_device(): block = lax.all_to_all(sent, 'frames', 0, 0)  21.4 us
    ppermute x7, starting transfers between devices, send(): lax.ppermute(piece, 'frames', [(i, i ^ k) for i in range(devices)])  9.77 us
    all_to_all x1, waiting for transfers between devices, per_device(): stats = lax.all_to_all(copies, ('rows', 'frames'), 0, 0)  9.21 us
    ppermute x7, waiting for transfers between devices, send(): lax.ppermute(piece, 'frames', [(i, i ^ k) for i in range(devices)])  7.98 us
    all_to_all x1, starting transfers between devices, per_device(): stats = lax.all_to_all(copies, ('rows', 'frames'), 0, 0)  7.66 us
    pallas_call x2, Pallas kernels, attend_rest(): pl.pallas_call(functools.partial(attend_rest_kernel, steps), out_shape=(p...  5.08 us
    pallas_call x1, Pallas kernels, attend_first(): pl.pallas_call(functools.partial(attend_first_kernel, steps, count, 4), o...  3.49 us
    pallas_call x1, Pallas kernels, upsample(): pl.pallas_call(functools.partial(upsample_kernel, share), out_shape=(jax....  2.54 us
  transfers between devices with their start and end apart: 8, of which 5 were waited for; matrix products, arithmetic and copies ran while one was open for 0% of the time, Pallas kernels for 7%

profile of v6, /device:TPU:0, one launch (start us, length us, event | category | flops | bytes accessed | tf_op | source)
XLA Modules:
  0.0 70.8 jit_solution(1998532571096662197)
XLA Ops:
  0.0 1.2 %copy-done.1 = bf16[16,104,256]{2,1,0:T(8,128)(2,1)S(1)} copy-done((bf16[16,104,256]{2,1,0:T(8,128)(2,1)S(1)}, bf16[16,104,256]{2,1,0:T(8,128)(2,1)}, u32[]{:S(2)}) %copy-start.1) | copy-done | bytes 851992
  1.2 0.7 %copy-done.4 = bf16[32,256]{1,0:T(8,128)(2,1)S(1)} copy-done((bf16[32,256]{1,0:T(8,128)(2,1)S(1)}, bf16[32,256]{1,0:T(8,128)(2,1)}, u32[]{:S(2)}) %copy-start.4) | copy-done | bytes 16408
  1.9 0.3 pack_latent.1
  2.2 0.0 copy-start
  2.2 0.0 copy-start.2
  2.2 21.4 %all_to_all.16.block_ref = bf16[8,240,256]{2,1,0:T(8,128)(2,1)S(1)} all-to-all(bf16[8,240,256]{2,1,0:T(8,128)(2,1)S(1)} %pack_latent.1), channel_id=1, replica_groups=mesh['rows'=16,'frames'=8] {'frames'}, dimensions={0} | all-to-all | bytes 1966080 | tf_op jit(solution)/shard_map/all_to_all | solution.py:353
  23.6 2.5 %upsample.1 = (bf16[13,2,128,256]{3,2,1,0:T(8,128)(2,1)S(1)}, f32[128,128]{1,0:T(8,128)}) custom-call(bf16[8,240,256]{2,1,0:T(8,128)(2,1)S(1)} %all_to_all.16.block_ref, bf16[4,256,256]{2,1,0:T(8,128)(2,1)S(1)} %copy-done.3), custom_call_target="tpu_custom_call" | custom-call | tf_op jit(solution)/shard_map/upsample/pallas_call | solution.py:139
  26.2 7.7 %all-to-all-start.1 = ((f32[128,1,128]{2,1,0:T(1,128)}), f32[128,1,128]{2,1,0:T(1,128)S(1)}, u32[]{:S(2)}, u32[]{:S(2)}) async-start(f32[128,1,128]{2,1,0:T(1,128)} %bitcast.1), calls=%async_computation.1 | async-start | bytes 131072 | tf_op jit(solution)/shard_map/all_to_all | solution.py:355
  33.9 9.2 %all-to-all-done.1 = f32[128,1,128]{2,1,0:T(1,128)S(1)} async-done(((f32[128,1,128]{2,1,0:T(1,128)}), f32[128,1,128]{2,1,0:T(1,128)S(1)}, u32[]{:S(2)}, u32[]{:S(2)}) %all-to-all-start.1) | async-done | bytes 65568 | tf_op jit(solution)/shard_map/all_to_all | solution.py:355
  43.1 3.5 %attend_first.1 = (bf16[13,2,16,256]{3,2,1,0:T(8,128)(2,1)S(1)}, bf16[13,2,16,256]{3,2,1,0:T(8,128)(2,1)S(1)}, bf16[3328,256]{1,0:T(8,128)(2,1)S(1)}, bf16[3328,512]{1,0:T(8,128)(2,1)S(1)}) custom-call(bf16[13,2,128,256]{3,2,1,0:T(8,128)(2,1)S(1)} %get-tuple-element.17.up_ref, f32[128,128]{1,0:T(8,128)S(1)} %bitcast.4, bf16[1,256]{1,0:T(2,128)(2,1)S(1)} %reshape.5.gain_ref, ...), custom_call_target="tpu_custom_call" | custom-call | flops 981467136 | bytes 851968 | tf_op jit(solution)/shard_map/attend_first/pallas_call | solution.py:271
  46.6 0.4 collective-permute-start
  47.0 1.5 %collective-permute-start.1 = (bf16[13,2,16,256]{3,2,1,0:T(8,128)(2,1)S(1)}, bf16[13,2,16,256]{3,2,1,0:T(8,128)(2,1)S(1)}, u32[]{:S(2)}, u32[]{:S(2)}) collective-permute-start(bf16[13,2,16,256]{3,2,1,0:T(8,128)(2,1)S(1)} %get-tuple-element.20), channel_id=1, source_target_pairs={{0,2},{1,3},{2,0},{3,1},{4,6},{5,7},{6,4},{7,5},{8,10},{9,11},{10,... | collective-permute-start | bytes 638984 | tf_op jit(solution)/shard_map/ppermute | solution.py:358
  48.5 1.9 %attend_rest.2 = (bf16[13,2,16,256]{3,2,1,0:T(8,128)(2,1)S(1)}, bf16[13,2,16,256]{3,2,1,0:T(8,128)(2,1)S(1)}) custom-call(bf16[13,2,128,256]{3,2,1,0:T(8,128)(2,1)S(1)} %get-tuple-element.17.up_ref, bf16[3328,256]{1,0:T(8,128)(2,1)S(1)} %get-tuple-element.21.normed_ref, bf16[3328,512]{1,0:T(8,128)(2,1)S(1)} %get-tuple-element.22.keyed, ...), custom_call_target="tpu_custom_call" | custom-call | flops 981467136 | bytes 851968 | tf_op jit(solution)/shard_map/attend_rest/pallas_call | solution.py:289
  50.4 3.2 %collective-permute-start.2 = (bf16[13,2,16,256]{3,2,1,0:T(8,128)(2,1)S(1)}, bf16[13,2,16,256]{3,2,1,0:T(8,128)(2,1)S(1)}, u32[]{:S(2)}, u32[]{:S(2)}) collective-permute-start(bf16[13,2,16,256]{3,2,1,0:T(8,128)(2,1)S(1)} %get-tuple-element.23), channel_id=1, source_target_pairs={{0,6},{1,7},{2,4},{3,5},{4,2},{5,3},{6,0},{7,1},{8,14},{9,15},{10,... | collective-permute-start | bytes 638984 | tf_op jit(solution)/shard_map/ppermute | solution.py:358
  53.6 0.8 %collective-permute-start.3 = (bf16[13,2,16,256]{3,2,1,0:T(8,128)(2,1)S(1)}, bf16[13,2,16,256]{3,2,1,0:T(8,128)(2,1)S(1)}, u32[]{:S(2)}, u32[]{:S(2)}) collective-permute-start(bf16[13,2,16,256]{3,2,1,0:T(8,128)(2,1)S(1)} %get-tuple-element.24), channel_id=1, source_target_pairs={{0,7},{1,6},{2,5},{3,4},{4,3},{5,2},{6,1},{7,0},{8,15},{9,14},{10,... | collective-permute-start | bytes 638984 | tf_op jit(solution)/shard_map/ppermute | solution.py:358
  54.4 3.2 %attend_rest.3 = (bf16[13,2,16,256]{3,2,1,0:T(8,128)(2,1)S(1)}, bf16[13,2,16,256]{3,2,1,0:T(8,128)(2,1)S(1)}, bf16[13,2,16,256]{3,2,1,0:T(8,128)(2,1)S(1)}, bf16[13,2,16,256]{3,2,1,0:T(8,128)(2,1)S(1)}) custom-call(bf16[13,2,128,256]{3,2,1,0:T(8,128)(2,1)S(1)} %get-tuple-element.17.up_ref, bf16[3328,256]{1,0:T(8,128)(2,1)S(1)} %get-tuple-element.21.normed_ref, ...), custom_call_target="tpu_custom_call" | custom-call | flops 1962934272 | bytes 1703936 | tf_op jit(solution)/shard_map/attend_rest/pallas_call | solution.py:289
  57.6 1.4 %collective-permute-start.4 = (bf16[13,2,16,256]{3,2,1,0:T(8,128)(2,1)S(1)}, bf16[13,2,16,256]{3,2,1,0:T(8,128)(2,1)S(1)}, u32[]{:S(2)}, u32[]{:S(2)}) collective-permute-start(bf16[13,2,16,256]{3,2,1,0:T(8,128)(2,1)S(1)} %get-tuple-element.25), channel_id=1, source_target_pairs={{0,5},{1,4},{2,7},{3,6},{4,1},{5,0},{6,3},{7,2},{8,13},{9,12},{10,... | collective-permute-start | bytes 638984 | tf_op jit(solution)/shard_map/ppermute | solution.py:358
  59.0 1.6 %collective-permute-start.5 = (bf16[13,2,16,256]{3,2,1,0:T(8,128)(2,1)S(1)}, bf16[13,2,16,256]{3,2,1,0:T(8,128)(2,1)S(1)}, u32[]{:S(2)}, u32[]{:S(2)}) collective-permute-start(bf16[13,2,16,256]{3,2,1,0:T(8,128)(2,1)S(1)} %get-tuple-element.26), channel_id=1, source_target_pairs={{0,1},{1,0},{2,3},{3,2},{4,5},{5,4},{6,7},{7,6},{8,9},{9,8},{10,11... | collective-permute-start | bytes 638984 | tf_op jit(solution)/shard_map/ppermute | solution.py:358
  60.6 1.6 %collective-permute-done.1.refs_1_ = bf16[13,2,16,256]{3,2,1,0:T(8,128)(2,1)S(1)} collective-permute-done((bf16[13,2,16,256]{3,2,1,0:T(8,128)(2,1)S(1)}, bf16[13,2,16,256]{3,2,1,0:T(8,128)(2,1)S(1)}, u32[]{:S(2)}, u32[]{:S(2)}) %collective-permute-start.1) | collective-permute-done | bytes 213024 | tf_op jit(solution)/shard_map/ppermute | solution.py:358
  62.2 0.8 %collective-permute-start.6 = (bf16[13,2,16,256]{3,2,1,0:T(8,128)(2,1)S(1)}, bf16[13,2,16,256]{3,2,1,0:T(8,128)(2,1)S(1)}, u32[]{:S(2)}, u32[]{:S(2)}) collective-permute-start(bf16[13,2,16,256]{3,2,1,0:T(8,128)(2,1)S(1)} %get-tuple-element.27), channel_id=1, source_target_pairs={{0,3},{1,2},{2,1},{3,0},{4,7},{5,6},{6,5},{7,4},{8,11},{9,10},{10,... | collective-permute-start | bytes 638984 | tf_op jit(solution)/shard_map/ppermute | solution.py:358
  63.1 2.8 %collective-permute-done.3.refs_3_ = bf16[13,2,16,256]{3,2,1,0:T(8,128)(2,1)S(1)} collective-permute-done((bf16[13,2,16,256]{3,2,1,0:T(8,128)(2,1)S(1)}, bf16[13,2,16,256]{3,2,1,0:T(8,128)(2,1)S(1)}, u32[]{:S(2)}, u32[]{:S(2)}) %collective-permute-start.3) | collective-permute-done | bytes 213024 | tf_op jit(solution)/shard_map/ppermute | solution.py:358
  65.9 3.0 %collective-permute-done.4.refs_4_ = bf16[13,2,16,256]{3,2,1,0:T(8,128)(2,1)S(1)} collective-permute-done((bf16[13,2,16,256]{3,2,1,0:T(8,128)(2,1)S(1)}, bf16[13,2,16,256]{3,2,1,0:T(8,128)(2,1)S(1)}, u32[]{:S(2)}, u32[]{:S(2)}) %collective-permute-start.4) | collective-permute-done | bytes 213024 | tf_op jit(solution)/shard_map/ppermute | solution.py:358
  68.9 0.5 collective-permute-done.5.refs_5_
  69.4 1.4 %unpack_output.1 = bf16[32,104,256]{2,1,0:T(8,128)(2,1)} custom-call(bf16[13,2,16,256]{3,2,1,0:T(8,128)(2,1)S(1)} %collective-permute-done.refs_0_, bf16[13,2,16,256]{3,2,1,0:T(8,128)(2,1)S(1)} %collective-permute-done.1.refs_1_, bf16[13,2,16,256]{3,2,1,0:T(8,128)(2,1)S(1)} %collective-permute-done.2.refs_2_, ...), custom_call_target="tpu_custom_call" | custom-call | tf_op jit(solution)/shard_map/unpack_output/pallas_call | solution.py:331
  (12 shorter events, 0.0 us)
Async XLA Ops:
  0.0 1.2 %copy-start.1 = (bf16[16,104,256]{2,1,0:T(8,128)(2,1)S(1)}, bf16[16,104,256]{2,1,0:T(8,128)(2,1)}, u32[]{:S(2)}) copy-start(bf16[16,104,256]{2,1,0:T(8,128)(2,1)} %latent_ref.1) | copy-start | bytes 2555908
  1.2 0.7 %copy-start.4 = (bf16[32,256]{1,0:T(8,128)(2,1)S(1)}, bf16[32,256]{1,0:T(8,128)(2,1)}, u32[]{:S(2)}) copy-start(bf16[32,256]{1,0:T(8,128)(2,1)} %embed_ref.1) | copy-start | bytes 49156
  1.9 21.7 %copy-start.3 = (bf16[4,256,256]{2,1,0:T(8,128)(2,1)S(1)}, bf16[4,256,256]{2,1,0:T(8,128)(2,1)}, u32[]{:S(2)}) copy-start(bf16[4,256,256]{2,1,0:T(8,128)(2,1)} %conv_ref.1) | copy-start | bytes 1572868
  2.2 31.7 %copy-start.5 = (bf16[256]{0:T(256)(128)(2,1)S(1)}, bf16[256]{0:T(256)(128)(2,1)}, u32[]{:S(2)}) copy-start(bf16[256]{0:T(256)(128)(2,1)} %param.8) | copy-start | bytes 1540
  2.2 40.9 %copy-start = (bf16[256,768]{1,0:T(8,128)(2,1)S(1)}, bf16[256,768]{1,0:T(8,128)(2,1)}, u32[]{:S(2)}) copy-start(bf16[256,768]{1,0:T(8,128)(2,1)} %qkv_ref.5) | copy-start | bytes 1179652
  2.2 40.9 %copy-start.2 = (bf16[256,256]{1,0:T(8,128)(2,1)S(1)}, bf16[256,256]{1,0:T(8,128)(2,1)}, u32[]{:S(2)}) copy-start(bf16[256,256]{1,0:T(8,128)(2,1)} %out_weight_ref.5) | copy-start | bytes 393220
  26.2 16.9 %all-to-all-start.1 = ((f32[128,1,128]{2,1,0:T(1,128)}), f32[128,1,128]{2,1,0:T(1,128)S(1)}, u32[]{:S(2)}, u32[]{:S(2)}) async-start(f32[128,1,128]{2,1,0:T(1,128)} %bitcast.1), calls=%async_computation.1 | async-start | bytes 131072 | tf_op jit(solution)/shard_map/all_to_all | solution.py:355
  46.6 12.4 %collective-permute-start = (bf16[13,2,16,256]{3,2,1,0:T(8,128)(2,1)S(1)}, bf16[13,2,16,256]{3,2,1,0:T(8,128)(2,1)S(1)}, u32[]{:S(2)}, u32[]{:S(2)}) collective-permute-start(bf16[13,2,16,256]{3,2,1,0:T(8,128)(2,1)S(1)} %get-tuple-element.19), channel_id=1, source_target_pairs={{0,4},{1,5},{2,6},{3,7},{4,0},{5,1},{6,2},{7,3},{8,12},{9,13},{10,... | collective-permute-start | bytes 638984 | tf_op jit(solution)/shard_map/ppermute | solution.py:358
  47.0 15.2 %collective-permute-start.1 = (bf16[13,2,16,256]{3,2,1,0:T(8,128)(2,1)S(1)}, bf16[13,2,16,256]{3,2,1,0:T(8,128)(2,1)S(1)}, u32[]{:S(2)}, u32[]{:S(2)}) collective-permute-start(bf16[13,2,16,256]{3,2,1,0:T(8,128)(2,1)S(1)} %get-tuple-element.20), channel_id=1, source_target_pairs={{0,2},{1,3},{2,0},{3,1},{4,6},{5,7},{6,4},{7,5},{8,10},{9,11},{10,... | collective-permute-start | bytes 638984 | tf_op jit(solution)/shard_map/ppermute | solution.py:358
  50.4 12.6 %collective-permute-start.2 = (bf16[13,2,16,256]{3,2,1,0:T(8,128)(2,1)S(1)}, bf16[13,2,16,256]{3,2,1,0:T(8,128)(2,1)S(1)}, u32[]{:S(2)}, u32[]{:S(2)}) collective-permute-start(bf16[13,2,16,256]{3,2,1,0:T(8,128)(2,1)S(1)} %get-tuple-element.23), channel_id=1, source_target_pairs={{0,6},{1,7},{2,4},{3,5},{4,2},{5,3},{6,0},{7,1},{8,14},{9,15},{10,... | collective-permute-start | bytes 638984 | tf_op jit(solution)/shard_map/ppermute | solution.py:358
  53.6 12.3 %collective-permute-start.3 = (bf16[13,2,16,256]{3,2,1,0:T(8,128)(2,1)S(1)}, bf16[13,2,16,256]{3,2,1,0:T(8,128)(2,1)S(1)}, u32[]{:S(2)}, u32[]{:S(2)}) collective-permute-start(bf16[13,2,16,256]{3,2,1,0:T(8,128)(2,1)S(1)} %get-tuple-element.24), channel_id=1, source_target_pairs={{0,7},{1,6},{2,5},{3,4},{4,3},{5,2},{6,1},{7,0},{8,15},{9,14},{10,... | collective-permute-start | bytes 638984 | tf_op jit(solution)/shard_map/ppermute | solution.py:358
  57.6 11.2 %collective-permute-start.4 = (bf16[13,2,16,256]{3,2,1,0:T(8,128)(2,1)S(1)}, bf16[13,2,16,256]{3,2,1,0:T(8,128)(2,1)S(1)}, u32[]{:S(2)}, u32[]{:S(2)}) collective-permute-start(bf16[13,2,16,256]{3,2,1,0:T(8,128)(2,1)S(1)} %get-tuple-element.25), channel_id=1, source_target_pairs={{0,5},{1,4},{2,7},{3,6},{4,1},{5,0},{6,3},{7,2},{8,13},{9,12},{10,... | collective-permute-start | bytes 638984 | tf_op jit(solution)/shard_map/ppermute | solution.py:358
  59.0 10.4 %collective-permute-start.5 = (bf16[13,2,16,256]{3,2,1,0:T(8,128)(2,1)S(1)}, bf16[13,2,16,256]{3,2,1,0:T(8,128)(2,1)S(1)}, u32[]{:S(2)}, u32[]{:S(2)}) collective-permute-start(bf16[13,2,16,256]{3,2,1,0:T(8,128)(2,1)S(1)} %get-tuple-element.26), channel_id=1, source_target_pairs={{0,1},{1,0},{2,3},{3,2},{4,5},{5,4},{6,7},{7,6},{8,9},{9,8},{10,11... | collective-permute-start | bytes 638984 | tf_op jit(solution)/shard_map/ppermute | solution.py:358
  62.2 7.2 %collective-permute-start.6 = (bf16[13,2,16,256]{3,2,1,0:T(8,128)(2,1)S(1)}, bf16[13,2,16,256]{3,2,1,0:T(8,128)(2,1)S(1)}, u32[]{:S(2)}, u32[]{:S(2)}) collective-permute-start(bf16[13,2,16,256]{3,2,1,0:T(8,128)(2,1)S(1)} %get-tuple-element.27), channel_id=1, source_target_pairs={{0,3},{1,2},{2,1},{3,0},{4,7},{5,6},{6,5},{7,4},{8,11},{9,10},{10,... | collective-permute-start | bytes 638984 | tf_op jit(solution)/shard_map/ppermute | solution.py:358

commit v7 on v6

--- a/solution.py
+++ b/solution.py
@@ -342,7 +342,7 @@
     )(*blocks)
 
 
-TARGETS = ((4, 2), (6, 7), (5, 1, 3, 0))
+TARGETS = ((4, 2), (6, 7), (5, 1, 3), (0,))
 
 
 def per_device(latent, conv_weight, norm_gain, frame_embed, qkv_weight, out_weight):

time: 71.1 us -> 71.2 us (level)
  Pallas kernels: 12.8 us -> 15.7 us
  waiting for transfers between devices: 17.2 us -> 14.9 us
    pallas_call x2 -> x3, Pallas kernels: 5.08 us -> 8.04 us  [attend_rest(): pl.pallas_call(functools.partial(attend_rest_kernel, steps), out_shape=(p...]
    ppermute x7, waiting for transfers between devices: 7.98 us -> 5.71 us  [send(): lax.ppermute(piece, 'frames', [(i, i ^ k) for i in range(devices)])]
    ppermute x7, starting transfers between devices: 9.77 us -> 9 us  [send(): lax.ppermute(piece, 'frames', [(i, i ^ k) for i in range(devices)])]
  transfers between devices with their start and end apart: 8 -> 8, of which waited for: 5 -> 5; matrix products, arithmetic and copies ran while one was open for 0% -> 0% of each run, Pallas kernels for 7% -> 11%
where the time goes in v7:
time: 71.2 us; the launch traced here: 70.9 us
  blocking collectives  21.4 us (30%)
  starting transfers between devices  16.7 us (23%)
  Pallas kernels  15.7 us (22%)
  waiting for transfers between devices  14.9 us (21%)
  local copies, waits for them, and re-layouts  1.9 us (3%)
    all_to_all x1, blocking collectives, per_device(): block = lax.all_to_all(sent, 'frames', 0, 0)  21.4 us
    all_to_all x1, waiting for transfers between devices, per_device(): stats = lax.all_to_all(copies, ('rows', 'frames'), 0, 0)  9.21 us
    ppermute x7, starting transfers between devices, send(): lax.ppermute(piece, 'frames', [(i, i ^ k) for i in range(devices)])  9 us
    pallas_call x3, Pallas kernels, attend_rest(): pl.pallas_call(functools.partial(attend_rest_kernel, steps), out_shape=(p...  8.04 us
    all_to_all x1, starting transfers between devices, per_device(): stats = lax.all_to_all(copies, ('rows', 'frames'), 0, 0)  7.66 us
    ppermute x7, waiting for transfers between devices, send(): lax.ppermute(piece, 'frames', [(i, i ^ k) for i in range(devices)])  5.71 us
    pallas_call x1, Pallas kernels, attend_first(): pl.pallas_call(functools.partial(attend_first_kernel, steps, count, 4), o...  3.49 us
    pallas_call x1, Pallas kernels, upsample(): pl.pallas_call(functools.partial(upsample_kernel, share), out_shape=(jax....  2.54 us
  transfers between devices with their start and end apart: 8, of which 5 were waited for; matrix products, arithmetic and copies ran while one was open for 0% of the time, Pallas kernels for 11%

profile of v7, /device:TPU:0, one launch (start us, length us, event | category | flops | bytes accessed | tf_op | source)
XLA Modules:
  0.0 70.9 jit_solution(3029132957146522648)
XLA Ops:
  0.0 1.2 %copy-done.2 = bf16[16,104,256]{2,1,0:T(8,128)(2,1)S(1)} copy-done((bf16[16,104,256]{2,1,0:T(8,128)(2,1)S(1)}, bf16[16,104,256]{2,1,0:T(8,128)(2,1)}, u32[]{:S(2)}) %copy-start.2) | copy-done | bytes 851992
  1.2 0.7 %copy-done.4 = bf16[32,256]{1,0:T(8,128)(2,1)S(1)} copy-done((bf16[32,256]{1,0:T(8,128)(2,1)S(1)}, bf16[32,256]{1,0:T(8,128)(2,1)}, u32[]{:S(2)}) %copy-start.4) | copy-done | bytes 16408
  1.9 0.3 pack_latent.1
  2.2 0.0 copy-start
  2.2 21.4 %all_to_all.16.block_ref = bf16[8,240,256]{2,1,0:T(8,128)(2,1)S(1)} all-to-all(bf16[8,240,256]{2,1,0:T(8,128)(2,1)S(1)} %pack_latent.1), channel_id=1, replica_groups=mesh['rows'=16,'frames'=8] {'frames'}, dimensions={0} | all-to-all | bytes 1966080 | tf_op jit(solution)/shard_map/all_to_all | solution.py:353
  23.6 2.5 %upsample.1 = (bf16[13,2,128,256]{3,2,1,0:T(8,128)(2,1)S(1)}, f32[128,128]{1,0:T(8,128)}) custom-call(bf16[8,240,256]{2,1,0:T(8,128)(2,1)S(1)} %all_to_all.16.block_ref, bf16[4,256,256]{2,1,0:T(8,128)(2,1)S(1)} %copy-done.3), custom_call_target="tpu_custom_call" | custom-call | tf_op jit(solution)/shard_map/upsample/pallas_call | solution.py:139
  26.2 7.7 %all-to-all-start.1 = ((f32[128,1,128]{2,1,0:T(1,128)}), f32[128,1,128]{2,1,0:T(1,128)S(1)}, u32[]{:S(2)}, u32[]{:S(2)}) async-start(f32[128,1,128]{2,1,0:T(1,128)} %bitcast.1), calls=%async_computation.1 | async-start | bytes 131072 | tf_op jit(solution)/shard_map/all_to_all | solution.py:355
  33.9 9.2 %all-to-all-done.1 = f32[128,1,128]{2,1,0:T(1,128)S(1)} async-done(((f32[128,1,128]{2,1,0:T(1,128)}), f32[128,1,128]{2,1,0:T(1,128)S(1)}, u32[]{:S(2)}, u32[]{:S(2)}) %all-to-all-start.1) | async-done | bytes 65568 | tf_op jit(solution)/shard_map/all_to_all | solution.py:355
  43.1 3.5 %attend_first.1 = (bf16[13,2,16,256]{3,2,1,0:T(8,128)(2,1)S(1)}, bf16[13,2,16,256]{3,2,1,0:T(8,128)(2,1)S(1)}, bf16[3328,256]{1,0:T(8,128)(2,1)S(1)}, bf16[3328,512]{1,0:T(8,128)(2,1)S(1)}) custom-call(bf16[13,2,128,256]{3,2,1,0:T(8,128)(2,1)S(1)} %get-tuple-element.16.up_ref, f32[128,128]{1,0:T(8,128)S(1)} %bitcast.4, bf16[1,256]{1,0:T(2,128)(2,1)S(1)} %reshape.5.gain_ref, ...), custom_call_target="tpu_custom_call" | custom-call | flops 981467136 | bytes 851968 | tf_op jit(solution)/shard_map/attend_first/pallas_call | solution.py:271
  46.6 0.5 collective-permute-start
  47.0 1.5 %collective-permute-start.1 = (bf16[13,2,16,256]{3,2,1,0:T(8,128)(2,1)S(1)}, bf16[13,2,16,256]{3,2,1,0:T(8,128)(2,1)S(1)}, u32[]{:S(2)}, u32[]{:S(2)}) collective-permute-start(bf16[13,2,16,256]{3,2,1,0:T(8,128)(2,1)S(1)} %get-tuple-element.19), channel_id=1, source_target_pairs={{0,2},{1,3},{2,0},{3,1},{4,6},{5,7},{6,4},{7,5},{8,10},{9,11},{10,... | collective-permute-start | bytes 638984 | tf_op jit(solution)/shard_map/ppermute | solution.py:358
  48.5 1.9 %attend_rest.3 = (bf16[13,2,16,256]{3,2,1,0:T(8,128)(2,1)S(1)}, bf16[13,2,16,256]{3,2,1,0:T(8,128)(2,1)S(1)}) custom-call(bf16[13,2,128,256]{3,2,1,0:T(8,128)(2,1)S(1)} %get-tuple-element.16.up_ref, bf16[3328,256]{1,0:T(8,128)(2,1)S(1)} %get-tuple-element.20.normed_ref, bf16[3328,512]{1,0:T(8,128)(2,1)S(1)} %get-tuple-element.21.keyed, ...), custom_call_target="tpu_custom_call" | custom-call | flops 981467136 | bytes 851968 | tf_op jit(solution)/shard_map/attend_rest/pallas_call | solution.py:289
  50.4 3.2 %collective-permute-start.2 = (bf16[13,2,16,256]{3,2,1,0:T(8,128)(2,1)S(1)}, bf16[13,2,16,256]{3,2,1,0:T(8,128)(2,1)S(1)}, u32[]{:S(2)}, u32[]{:S(2)}) collective-permute-start(bf16[13,2,16,256]{3,2,1,0:T(8,128)(2,1)S(1)} %get-tuple-element.22), channel_id=1, source_target_pairs={{0,6},{1,7},{2,4},{3,5},{4,2},{5,3},{6,0},{7,1},{8,14},{9,15},{10,... | collective-permute-start | bytes 638984 | tf_op jit(solution)/shard_map/ppermute | solution.py:358
  53.6 0.8 %collective-permute-start.3 = (bf16[13,2,16,256]{3,2,1,0:T(8,128)(2,1)S(1)}, bf16[13,2,16,256]{3,2,1,0:T(8,128)(2,1)S(1)}, u32[]{:S(2)}, u32[]{:S(2)}) collective-permute-start(bf16[13,2,16,256]{3,2,1,0:T(8,128)(2,1)S(1)} %get-tuple-element.23), channel_id=1, source_target_pairs={{0,7},{1,6},{2,5},{3,4},{4,3},{5,2},{6,1},{7,0},{8,15},{9,14},{10,... | collective-permute-start | bytes 638984 | tf_op jit(solution)/shard_map/ppermute | solution.py:358
  54.4 2.5 %attend_rest.4 = (bf16[13,2,16,256]{3,2,1,0:T(8,128)(2,1)S(1)}, bf16[13,2,16,256]{3,2,1,0:T(8,128)(2,1)S(1)}, bf16[13,2,16,256]{3,2,1,0:T(8,128)(2,1)S(1)}) custom-call(bf16[13,2,128,256]{3,2,1,0:T(8,128)(2,1)S(1)} %get-tuple-element.16.up_ref, bf16[3328,256]{1,0:T(8,128)(2,1)S(1)} %get-tuple-element.20.normed_ref, ...), custom_call_target="tpu_custom_call" | custom-call | flops 1472200704 | bytes 1277952 | tf_op jit(solution)/shard_map/attend_rest/pallas_call | solution.py:289
  56.9 1.4 %collective-permute-start.4 = (bf16[13,2,16,256]{3,2,1,0:T(8,128)(2,1)S(1)}, bf16[13,2,16,256]{3,2,1,0:T(8,128)(2,1)S(1)}, u32[]{:S(2)}, u32[]{:S(2)}) collective-permute-start(bf16[13,2,16,256]{3,2,1,0:T(8,128)(2,1)S(1)} %get-tuple-element.24), channel_id=1, source_target_pairs={{0,5},{1,4},{2,7},{3,6},{4,1},{5,0},{6,3},{7,2},{8,13},{9,12},{10,... | collective-permute-start | bytes 638984 | tf_op jit(solution)/shard_map/ppermute | solution.py:358
  58.3 1.6 %collective-permute-start.5 = (bf16[13,2,16,256]{3,2,1,0:T(8,128)(2,1)S(1)}, bf16[13,2,16,256]{3,2,1,0:T(8,128)(2,1)S(1)}, u32[]{:S(2)}, u32[]{:S(2)}) collective-permute-start(bf16[13,2,16,256]{3,2,1,0:T(8,128)(2,1)S(1)} %get-tuple-element.25), channel_id=1, source_target_pairs={{0,1},{1,0},{2,3},{3,2},{4,5},{5,4},{6,7},{7,6},{8,9},{9,8},{10,11... | collective-permute-start | bytes 638984 | tf_op jit(solution)/shard_map/ppermute | solution.py:358
  59.9 2.4 %collective-permute-done.1.refs_1_ = bf16[13,2,16,256]{3,2,1,0:T(8,128)(2,1)S(1)} collective-permute-done((bf16[13,2,16,256]{3,2,1,0:T(8,128)(2,1)S(1)}, bf16[13,2,16,256]{3,2,1,0:T(8,128)(2,1)S(1)}, u32[]{:S(2)}, u32[]{:S(2)}) %collective-permute-start.1) | collective-permute-done | bytes 213024 | tf_op jit(solution)/shard_map/ppermute | solution.py:358
  62.3 0.1 collective-permute-start.6
  62.3 3.7 %attend_rest.5.refs_7_ = bf16[13,2,16,256]{3,2,1,0:T(8,128)(2,1)S(1)} custom-call(bf16[13,2,128,256]{3,2,1,0:T(8,128)(2,1)S(1)} %get-tuple-element.16.up_ref, bf16[3328,256]{1,0:T(8,128)(2,1)S(1)} %get-tuple-element.20.normed_ref, bf16[3328,512]{1,0:T(8,128)(2,1)S(1)} %get-tuple-element.21.keyed, bf16[256,768]{1,0:T(8,128)(2,1)S(1)} %copy-done, ...), custom_call_target="tpu_custom_call" | custom-call | flops 490733568 | bytes 425984 | tf_op jit(solution)/shard_map/attend_rest/pallas_call | solution.py:289
  66.0 2.9 %collective-permute-done.4.refs_4_ = bf16[13,2,16,256]{3,2,1,0:T(8,128)(2,1)S(1)} collective-permute-done((bf16[13,2,16,256]{3,2,1,0:T(8,128)(2,1)S(1)}, bf16[13,2,16,256]{3,2,1,0:T(8,128)(2,1)S(1)}, u32[]{:S(2)}, u32[]{:S(2)}) %collective-permute-start.4) | collective-permute-done | bytes 213024 | tf_op jit(solution)/shard_map/ppermute | solution.py:358
  68.9 0.1 collective-permute-done.5.refs_5_
  68.9 0.4 collective-permute-done.6.refs_6_
  69.4 1.4 %unpack_output.1 = bf16[32,104,256]{2,1,0:T(8,128)(2,1)} custom-call(bf16[13,2,16,256]{3,2,1,0:T(8,128)(2,1)S(1)} %collective-permute-done.refs_0_, bf16[13,2,16,256]{3,2,1,0:T(8,128)(2,1)S(1)} %collective-permute-done.1.refs_1_, bf16[13,2,16,256]{3,2,1,0:T(8,128)(2,1)S(1)} %collective-permute-done.2.refs_2_, ...), custom_call_target="tpu_custom_call" | custom-call | tf_op jit(solution)/shard_map/unpack_output/pallas_call | solution.py:331
  (13 shorter events, 0.0 us)
Async XLA Ops:
  0.0 1.2 %copy-start.2 = (bf16[16,104,256]{2,1,0:T(8,128)(2,1)S(1)}, bf16[16,104,256]{2,1,0:T(8,128)(2,1)}, u32[]{:S(2)}) copy-start(bf16[16,104,256]{2,1,0:T(8,128)(2,1)} %latent_ref.1) | copy-start | bytes 2555908
  1.2 0.7 %copy-start.4 = (bf16[32,256]{1,0:T(8,128)(2,1)S(1)}, bf16[32,256]{1,0:T(8,128)(2,1)}, u32[]{:S(2)}) copy-start(bf16[32,256]{1,0:T(8,128)(2,1)} %embed_ref.1) | copy-start | bytes 49156
  1.9 21.7 %copy-start.3 = (bf16[4,256,256]{2,1,0:T(8,128)(2,1)S(1)}, bf16[4,256,256]{2,1,0:T(8,128)(2,1)}, u32[]{:S(2)}) copy-start(bf16[4,256,256]{2,1,0:T(8,128)(2,1)} %conv_ref.1) | copy-start | bytes 1572868
  2.2 31.7 %copy-start.5 = (bf16[256]{0:T(256)(128)(2,1)S(1)}, bf16[256]{0:T(256)(128)(2,1)}, u32[]{:S(2)}) copy-start(bf16[256]{0:T(256)(128)(2,1)} %param.8) | copy-start | bytes 1540
  2.2 40.9 %copy-start = (bf16[256,768]{1,0:T(8,128)(2,1)S(1)}, bf16[256,768]{1,0:T(8,128)(2,1)}, u32[]{:S(2)}) copy-start(bf16[256,768]{1,0:T(8,128)(2,1)} %qkv_ref.7) | copy-start | bytes 1179652
  2.2 40.9 %copy-start.1 = (bf16[256,256]{1,0:T(8,128)(2,1)S(1)}, bf16[256,256]{1,0:T(8,128)(2,1)}, u32[]{:S(2)}) copy-start(bf16[256,256]{1,0:T(8,128)(2,1)} %out_weight_ref.7) | copy-start | bytes 393220
  26.2 16.9 %all-to-all-start.1 = ((f32[128,1,128]{2,1,0:T(1,128)}), f32[128,1,128]{2,1,0:T(1,128)S(1)}, u32[]{:S(2)}, u32[]{:S(2)}) async-start(f32[128,1,128]{2,1,0:T(1,128)} %bitcast.1), calls=%async_computation.1 | async-start | bytes 131072 | tf_op jit(solution)/shard_map/all_to_all | solution.py:355
  46.6 11.7 %collective-permute-start = (bf16[13,2,16,256]{3,2,1,0:T(8,128)(2,1)S(1)}, bf16[13,2,16,256]{3,2,1,0:T(8,128)(2,1)S(1)}, u32[]{:S(2)}, u32[]{:S(2)}) collective-permute-start(bf16[13,2,16,256]{3,2,1,0:T(8,128)(2,1)S(1)} %get-tuple-element.18), channel_id=1, source_target_pairs={{0,4},{1,5},{2,6},{3,7},{4,0},{5,1},{6,2},{7,3},{8,12},{9,13},{10,... | collective-permute-start | bytes 638984 | tf_op jit(solution)/shard_map/ppermute | solution.py:358
  47.0 15.2 %collective-permute-start.1 = (bf16[13,2,16,256]{3,2,1,0:T(8,128)(2,1)S(1)}, bf16[13,2,16,256]{3,2,1,0:T(8,128)(2,1)S(1)}, u32[]{:S(2)}, u32[]{:S(2)}) collective-permute-start(bf16[13,2,16,256]{3,2,1,0:T(8,128)(2,1)S(1)} %get-tuple-element.19), channel_id=1, source_target_pairs={{0,2},{1,3},{2,0},{3,1},{4,6},{5,7},{6,4},{7,5},{8,10},{9,11},{10,... | collective-permute-start | bytes 638984 | tf_op jit(solution)/shard_map/ppermute | solution.py:358
  50.4 15.6 %collective-permute-start.2 = (bf16[13,2,16,256]{3,2,1,0:T(8,128)(2,1)S(1)}, bf16[13,2,16,256]{3,2,1,0:T(8,128)(2,1)S(1)}, u32[]{:S(2)}, u32[]{:S(2)}) collective-permute-start(bf16[13,2,16,256]{3,2,1,0:T(8,128)(2,1)S(1)} %get-tuple-element.22), channel_id=1, source_target_pairs={{0,6},{1,7},{2,4},{3,5},{4,2},{5,3},{6,0},{7,1},{8,14},{9,15},{10,... | collective-permute-start | bytes 638984 | tf_op jit(solution)/shard_map/ppermute | solution.py:358
  53.6 12.4 %collective-permute-start.3 = (bf16[13,2,16,256]{3,2,1,0:T(8,128)(2,1)S(1)}, bf16[13,2,16,256]{3,2,1,0:T(8,128)(2,1)S(1)}, u32[]{:S(2)}, u32[]{:S(2)}) collective-permute-start(bf16[13,2,16,256]{3,2,1,0:T(8,128)(2,1)S(1)} %get-tuple-element.23), channel_id=1, source_target_pairs={{0,7},{1,6},{2,5},{3,4},{4,3},{5,2},{6,1},{7,0},{8,15},{9,14},{10,... | collective-permute-start | bytes 638984 | tf_op jit(solution)/shard_map/ppermute | solution.py:358
  56.9 12.0 %collective-permute-start.4 = (bf16[13,2,16,256]{3,2,1,0:T(8,128)(2,1)S(1)}, bf16[13,2,16,256]{3,2,1,0:T(8,128)(2,1)S(1)}, u32[]{:S(2)}, u32[]{:S(2)}) collective-permute-start(bf16[13,2,16,256]{3,2,1,0:T(8,128)(2,1)S(1)} %get-tuple-element.24), channel_id=1, source_target_pairs={{0,5},{1,4},{2,7},{3,6},{4,1},{5,0},{6,3},{7,2},{8,13},{9,12},{10,... | collective-permute-start | bytes 638984 | tf_op jit(solution)/shard_map/ppermute | solution.py:358
  58.3 10.7 %collective-permute-start.5 = (bf16[13,2,16,256]{3,2,1,0:T(8,128)(2,1)S(1)}, bf16[13,2,16,256]{3,2,1,0:T(8,128)(2,1)S(1)}, u32[]{:S(2)}, u32[]{:S(2)}) collective-permute-start(bf16[13,2,16,256]{3,2,1,0:T(8,128)(2,1)S(1)} %get-tuple-element.25), channel_id=1, source_target_pairs={{0,1},{1,0},{2,3},{3,2},{4,5},{5,4},{6,7},{7,6},{8,9},{9,8},{10,11... | collective-permute-start | bytes 638984 | tf_op jit(solution)/shard_map/ppermute | solution.py:358
  62.3 7.1 %collective-permute-start.6 = (bf16[13,2,16,256]{3,2,1,0:T(8,128)(2,1)S(1)}, bf16[13,2,16,256]{3,2,1,0:T(8,128)(2,1)S(1)}, u32[]{:S(2)}, u32[]{:S(2)}) collective-permute-start(bf16[13,2,16,256]{3,2,1,0:T(8,128)(2,1)S(1)} %get-tuple-element.26), channel_id=1, source_target_pairs={{0,3},{1,2},{2,1},{3,0},{4,7},{5,6},{6,5},{7,4},{8,11},{9,10},{10,... | collective-permute-start | bytes 638984 | tf_op jit(solution)/shard_map/ppermute | solution.py:358
